TPU v7x, 32 devices: a whole 2x2x4 slice. The times are simulated.
32 devices in a mesh: batch: 8 (over y, x, core), seq: 4 (over z).
Axes of the slice: x: 2, y: 2, z: 4, core: 2. Of those that a mesh axis runs over, the one named last changes fastest.
Arguments:
- tokens: bfloat16 [32, 1024, 768], P('batch', 'seq'), may hold values from -6 to 6
- norm1_gain: bfloat16 [768], replicated, may hold values from 0.5 to 1.5
- w_query: bfloat16 [768, 768], replicated, may hold values from -0.078125 to 0.078125
- w_key: bfloat16 [768, 768], replicated, may hold values from -0.078125 to 0.078125
- w_value: bfloat16 [768, 768], replicated, may hold values from -0.21875 to 0.21875
- rel_bias: bfloat16 [32, 12], replicated, may hold values from -4 to 4
- w_output: bfloat16 [768, 768], replicated, may hold values from -0.875 to 0.875
- norm2_gain: bfloat16 [768], replicated, may hold values from 0.5 to 1.5
- w_in: bfloat16 [768, 3072], replicated, may hold values from -0.21875 to 0.21875
- w_out: bfloat16 [3072, 768], replicated, may hold values from -0.15625 to 0.15625
- final_gain: bfloat16 [768], replicated, may hold values from 0.5 to 1.5
- w_proj: bfloat16 [768, 768], replicated, may hold values from -0.21875 to 0.21875
- lengths: int32 [32, 16], P('batch'), may hold values from 1 to 256, 1024 in all within a row
- partner: int32 [512], P('batch'), may hold values from 0 to 511, as said below
- cotangent: bfloat16 [32, 1024, 768], P('batch', 'seq'), may hold values from -6 to 6
Outputs:
- block_out: bfloat16 [32, 1024, 768], P('batch', 'seq')
- embeddings: float32 [512, 768], P('batch')
- sentence_loss: float32 [512], P('batch')
- tokens_grad: float32 [32, 1024, 768], P('batch', 'seq')
- norm1_gain_grad: float32 [768], replicated
- query_grad: float32 [768, 768], P('seq', 'batch')
- key_grad: float32 [768, 768], P('seq', 'batch')
- value_grad: float32 [768, 768], P('seq', 'batch')
- rel_bias_grad: float32 [32, 12], replicated
- output_grad: float32 [768, 768], P('seq', 'batch')
- norm2_gain_grad: float32 [768], replicated
- in_grad: float32 [768, 3072], P('seq', 'batch')
- out_grad: float32 [3072, 768], P('seq', 'batch')
- final_gain_grad: float32 [768], replicated
- proj_grad: float32 [768, 768], P('seq', 'batch')
Inputs may be any that keep to these rules, and one draw needn't show every extreme that they name: Each row's 16 lengths sum to 1024, and every row's longest sentence has exactly 256 tokens. Pairs are mutual and never a sentence with itself: partner[partner[i]] == i and partner[i] != i.
All inputs are finite; a program needn't handle non-finite values.
Results may differ from a plain program's by a relative error of at most 0.017.
Values may be sent and summed in bfloat16 or wider, within the bound.
No kernel may reach another device: no remote copies, remote signals or barrier semaphores. Data moves between devices by JAX's collectives and lax.ppermute only.
A program may use at most 320 MiB of HBM per device.

v0:
```python
import jax
import jax.numpy as jnp
from jax import lax
from jax.sharding import PartitionSpec as P

EPS = 1e-06
NEGATIVE = -1e30
SHARPNESS = 50.0
THRESHOLDS = (12, 16, 23, 32, 46, 64, 91)
HIGHEST = lax.Precision.HIGHEST


def padded(block, sides, width):
    for axis, dim in sides:
        count = lax.axis_size(axis)
        forward = [(i, i + 1) for i in range(count - 1)]
        backward = [(target, source) for source, target in forward]
        low = lax.ppermute(
            lax.slice_in_dim(block, block.shape[dim] - width, None, axis=dim), axis, forward
        )
        high = lax.ppermute(lax.slice_in_dim(block, 0, width, axis=dim), axis, backward)
        block = jnp.concatenate([low, block, high], axis=dim)
    return block


def shifted(block, axis, distance):
    devices = range(lax.axis_size(axis))
    route = [(i - distance, i) for i in devices if i - distance in devices]
    return lax.ppermute(block, axis, route)


def bucket_of(offset):
    distance = jnp.abs(offset)
    beyond = jnp.zeros_like(distance)
    for threshold in THRESHOLDS:
        beyond = beyond + (distance >= threshold).astype(jnp.int32)
    within = jnp.where(distance < 8, distance, 8 + beyond)
    return within + 16 * (offset > 0).astype(jnp.int32)


def segment_of(seg_ends, where_pos):
    return jnp.sum((seg_ends[:, None, :] <= where_pos[None, :, None]).astype(jnp.int32), axis=-1)


def rms_scale(values):
    return lax.rsqrt(jnp.mean(values * values, axis=-1, keepdims=True) + EPS)


def rms_back(values, scale, grad_normed):
    return scale * (
        grad_normed
        - values * scale * scale * jnp.mean(grad_normed * values, axis=-1, keepdims=True)
    )


def gelu_tanh(values):
    return jax.nn.gelu(values, approximate=True)


def scores_of(block_q, block_k, same_seg, bias_grid):
    raw_dot = jnp.einsum("bihe,bjhe->bhij", block_q, block_k, preferred_element_type=jnp.float32)
    return jnp.where(same_seg[:, None], raw_dot + bias_grid[None], NEGATIVE)


def attend(block_q, block_k, block_v, same_seg, bias_grid):
    scores = scores_of(block_q, block_k, same_seg, bias_grid)
    row_peak = jnp.max(scores, axis=-1, keepdims=True)
    powers = jnp.exp(scores - row_peak)
    totals = jnp.sum(powers, axis=-1, keepdims=True)
    soft_probs = (powers / totals).astype(jnp.bfloat16)
    attended = jnp.einsum(
        "bhij,bjhe->bihe", soft_probs, block_v, preferred_element_type=jnp.float32
    )
    return (attended.astype(jnp.bfloat16), row_peak + jnp.log(totals))


def attend_back(block_q, block_k, block_v, same_seg, bias_grid, grad_mixed, logsum):
    scores = scores_of(block_q, block_k, same_seg, bias_grid)
    soft_probs = jnp.exp(scores - logsum)
    grad_probs = jnp.einsum(
        "bihe,bjhe->bhij", grad_mixed, block_v, preferred_element_type=jnp.float32
    )
    inner_sum = jnp.sum(soft_probs * grad_probs, axis=-1, keepdims=True)
    grad_scores = soft_probs * (grad_probs - inner_sum)
    grad_low = grad_scores.astype(jnp.bfloat16)
    grad_query = jnp.einsum(
        "bhij,bjhe->bihe", grad_low, block_k, preferred_element_type=jnp.float32
    )
    grad_key = jnp.einsum("bhij,bihe->bjhe", grad_low, block_q, preferred_element_type=jnp.float32)
    grad_value = jnp.einsum(
        "bhij,bihe->bjhe",
        soft_probs.astype(jnp.bfloat16),
        grad_mixed,
        preferred_element_type=jnp.float32,
    )
    return (grad_query.astype(jnp.bfloat16), grad_key, grad_value, jnp.sum(grad_scores, axis=0))


def shards(
    tokens,
    norm1_gain,
    w_query,
    w_key,
    w_value,
    rel_bias,
    w_output,
    norm2_gain,
    w_in,
    w_out,
    final_gain,
    w_proj,
    lengths,
    partner,
    cotangent,
):
    row_count, shard_len, model_dim = tokens.shape
    bucket_count, head_count = rel_bias.shape
    head_size = model_dim // head_count
    slot_count = lengths.shape[1]
    seq_count = lax.axis_size("seq")
    seq_place = lax.axis_index("seq")
    full_len = shard_len * seq_count
    tok_count = row_count * shard_len
    row_block = max(1, min(row_count, 512 // shard_len))
    block_count = row_count // row_block

    def by_blocks(array):
        return array.reshape((block_count, row_block) + array.shape[1:])

    inputs = tokens.astype(jnp.float32).reshape(tok_count, model_dim)
    gain_one = norm1_gain.astype(jnp.float32)
    gain_two = norm2_gain.astype(jnp.float32)
    gain_fin = final_gain.astype(jnp.float32)
    scale_one = rms_scale(inputs)
    normed_one = (inputs * scale_one * gain_one).astype(jnp.bfloat16)
    query_proj = jnp.dot(normed_one, w_query, preferred_element_type=jnp.float32).astype(
        jnp.bfloat16
    )
    key_proj = jnp.dot(normed_one, w_key, preferred_element_type=jnp.float32).astype(jnp.bfloat16)
    value_proj = jnp.dot(normed_one, w_value, preferred_element_type=jnp.float32).astype(
        jnp.bfloat16
    )
    stacked = jnp.stack([key_proj, value_proj]).reshape(2, row_count, shard_len, model_dim)
    rim_kv = padded(stacked, (("seq", 2),), shard_len)
    seg_ends = jnp.cumsum(lengths, axis=1)
    query_pos = seq_place * shard_len + jnp.arange(shard_len, dtype=jnp.int32)
    key_pos = (seq_place - 1) * shard_len + jnp.arange(3 * shard_len, dtype=jnp.int32)
    query_seg = segment_of(seg_ends, query_pos)
    key_seg = segment_of(seg_ends, key_pos)
    inside = (key_pos >= 0) & (key_pos < full_len)
    same_seg = (query_seg[:, :, None] == key_seg[:, None, :]) & inside[None, None, :]
    offsets = (
        jnp.arange(3 * shard_len, dtype=jnp.int32)[None, :]
        - shard_len
        - jnp.arange(shard_len, dtype=jnp.int32)[:, None]
    )
    bucket_hot = (
        bucket_of(offsets)[:, :, None] == jnp.arange(bucket_count, dtype=jnp.int32)[None, None, :]
    ).astype(jnp.bfloat16)
    bias_grid = jnp.einsum("ijc,ch->hij", bucket_hot, rel_bias, preferred_element_type=jnp.float32)
    blocks_q = by_blocks(query_proj.reshape(row_count, shard_len, head_count, head_size))
    blocks_mask = by_blocks(same_seg)

    def forward_block(pieces):
        return attend(pieces[0], pieces[1], pieces[2], pieces[3], bias_grid)

    blocks_k = by_blocks(rim_kv[0].reshape(row_count, 3 * shard_len, head_count, head_size))
    blocks_v = by_blocks(rim_kv[1].reshape(row_count, 3 * shard_len, head_count, head_size))
    attended, logsum = lax.map(forward_block, (blocks_q, blocks_k, blocks_v, blocks_mask))
    attended = attended.reshape(tok_count, model_dim)
    after_attn = inputs + jnp.dot(attended, w_output, preferred_element_type=jnp.float32)
    scale_two = rms_scale(after_attn)
    normed_two = (after_attn * scale_two * gain_two).astype(jnp.bfloat16)
    pre_act = jnp.dot(normed_two, w_in, preferred_element_type=jnp.float32)
    act_out = gelu_tanh(pre_act).astype(jnp.bfloat16)
    block_out = (after_attn + jnp.dot(act_out, w_out, preferred_element_type=jnp.float32)).astype(
        jnp.bfloat16
    )
    out_float = block_out.astype(jnp.float32)
    scale_fin = rms_scale(out_float)
    final_norm = out_float * scale_fin * gain_fin
    member = (
        query_seg[:, :, None] == jnp.arange(slot_count, dtype=jnp.int32)[None, None, :]
    ).astype(jnp.float32)
    partial_sums = jnp.einsum(
        "rts,rtd->rsd",
        member,
        final_norm.reshape(row_count, shard_len, model_dim),
        precision=HIGHEST,
    )
    pooled_sum = lax.psum(partial_sums, "seq")
    counts = lengths.astype(jnp.float32)[:, :, None]
    local_n = row_count * slot_count
    pooled = (pooled_sum / counts).reshape(local_n, model_dim)
    proj_float = w_proj.astype(jnp.float32)
    raw_emb = jnp.dot(pooled, proj_float, precision=HIGHEST)
    inv_norm = lax.rsqrt(jnp.sum(raw_emb * raw_emb, axis=-1, keepdims=True) + EPS)
    embedded = raw_emb * inv_norm
    everyone = lax.all_gather(embedded, "batch", axis=0, tiled=True)
    own_index = lax.axis_index("batch") * local_n + jnp.arange(local_n, dtype=jnp.int32)
    columns = jnp.arange(everyone.shape[0], dtype=jnp.int32)
    logits = SHARPNESS * jnp.einsum("nd,md->nm", embedded, everyone, precision=HIGHEST)
    logits = jnp.where(columns[None, :] == own_index[:, None], NEGATIVE, logits)
    row_peak = jnp.max(logits, axis=-1, keepdims=True)
    powers = jnp.exp(logits - row_peak)
    totals = jnp.sum(powers, axis=-1, keepdims=True)
    log_total = row_peak[:, 0] + jnp.log(totals[:, 0])
    is_target = columns[None, :] == partner[:, None]
    target_float = is_target.astype(jnp.float32)
    picked = jnp.sum(jnp.where(is_target, logits, 0.0), axis=-1)
    sent_loss = log_total - picked
    grad_logits = SHARPNESS * (powers / totals - target_float)
    grad_local = jnp.dot(grad_logits, everyone, precision=HIGHEST)
    grad_everyone = jnp.einsum("nm,nd->md", grad_logits, embedded, precision=HIGHEST)
    grad_returned = lax.psum_scatter(grad_everyone, "batch", scatter_dimension=0, tiled=True)
    grad_emb = grad_local + grad_returned
    grad_raw = inv_norm * (
        grad_emb - embedded * jnp.sum(embedded * grad_emb, axis=-1, keepdims=True)
    )
    lead_only = (seq_place == 0).astype(jnp.float32)
    grad_proj = lead_only * jnp.einsum("nd,ne->de", pooled, grad_raw, precision=HIGHEST)
    grad_pooled = jnp.einsum("ne,de->nd", grad_raw, proj_float, precision=HIGHEST)
    grad_pool_sum = grad_pooled.reshape(row_count, slot_count, model_dim) / counts
    grad_final = jnp.einsum("rts,rsd->rtd", member, grad_pool_sum, precision=HIGHEST).reshape(
        tok_count, model_dim
    )
    grad_gain_fin = jnp.sum(grad_final * out_float * scale_fin, axis=0)
    grad_out = rms_back(out_float, scale_fin, grad_final * gain_fin) + cotangent.astype(
        jnp.float32
    ).reshape(tok_count, model_dim)
    grad_branch = grad_out.astype(jnp.bfloat16)
    grad_w_out = jnp.einsum("tf,td->fd", act_out, grad_branch, preferred_element_type=jnp.float32)
    grad_hidden = jnp.einsum("td,fd->tf", grad_branch, w_out, preferred_element_type=jnp.float32)
    gelu_pullback = jax.vjp(gelu_tanh, pre_act)[1]
    grad_pre = gelu_pullback(grad_hidden)[0].astype(jnp.bfloat16)
    grad_w_in = jnp.einsum("td,tf->df", normed_two, grad_pre, preferred_element_type=jnp.float32)
    grad_normed_two = jnp.einsum("tf,df->td", grad_pre, w_in, preferred_element_type=jnp.float32)
    grad_gain_two = jnp.sum(grad_normed_two * after_attn * scale_two, axis=0)
    grad_after = grad_out + rms_back(after_attn, scale_two, grad_normed_two * gain_two)
    grad_attn = grad_after.astype(jnp.bfloat16)
    grad_w_output = jnp.einsum("td,te->de", attended, grad_attn, preferred_element_type=jnp.float32)
    grad_mixed = jnp.einsum(
        "te,de->td", grad_attn, w_output, preferred_element_type=jnp.float32
    ).astype(jnp.bfloat16)
    back_k = by_blocks(rim_kv[0].reshape(row_count, 3 * shard_len, head_count, head_size))
    back_v = by_blocks(rim_kv[1].reshape(row_count, 3 * shard_len, head_count, head_size))
    blocks_grad = by_blocks(grad_mixed.reshape(row_count, shard_len, head_count, head_size))

    def backward_block(pieces):
        return attend_back(
            pieces[0], pieces[1], pieces[2], pieces[3], bias_grid, pieces[4], pieces[5]
        )

    grad_q, grad_k, grad_v, grad_bias = lax.map(
        backward_block, (blocks_q, back_k, back_v, blocks_mask, blocks_grad, logsum)
    )
    grad_rel = jnp.einsum(
        "hij,ijc->ch", jnp.sum(grad_bias, axis=0), bucket_hot.astype(jnp.float32), precision=HIGHEST
    )
    grad_rim = jnp.stack(
        [
            grad_k.reshape(row_count, 3 * shard_len, model_dim),
            grad_v.reshape(row_count, 3 * shard_len, model_dim),
        ]
    )
    lower_part = grad_rim[:, :, :shard_len]
    upper_part = grad_rim[:, :, 2 * shard_len :]
    from_above = shifted(lower_part.astype(jnp.bfloat16), "seq", -1).astype(lower_part.dtype)
    from_below = shifted(upper_part.astype(jnp.bfloat16), "seq", 1).astype(upper_part.dtype)
    owned = grad_rim[:, :, shard_len : 2 * shard_len] + from_above + from_below
    grad_key = owned[0].reshape(tok_count, model_dim).astype(jnp.bfloat16)
    grad_value = owned[1].reshape(tok_count, model_dim).astype(jnp.bfloat16)
    grad_query = grad_q.reshape(tok_count, model_dim)
    grad_w_query = jnp.einsum(
        "td,te->de", normed_one, grad_query, preferred_element_type=jnp.float32
    )
    grad_w_key = jnp.einsum("td,te->de", normed_one, grad_key, preferred_element_type=jnp.float32)
    grad_w_value = jnp.einsum(
        "td,te->de", normed_one, grad_value, preferred_element_type=jnp.float32
    )
    grad_normed_one = jnp.einsum(
        "te,de->td", grad_query, w_query, preferred_element_type=jnp.float32
    )
    grad_normed_one = grad_normed_one + jnp.einsum(
        "te,de->td", grad_key, w_key, preferred_element_type=jnp.float32
    )
    grad_normed_one = grad_normed_one + jnp.einsum(
        "te,de->td", grad_value, w_value, preferred_element_type=jnp.float32
    )
    grad_gain_one = jnp.sum(grad_normed_one * inputs * scale_one, axis=0)
    grad_tokens = grad_after + rms_back(inputs, scale_one, grad_normed_one * gain_one)
    partial_mats = (
        lax.psum_scatter(grad_w_query, "batch", scatter_dimension=1, tiled=True),
        lax.psum_scatter(grad_w_key, "batch", scatter_dimension=1, tiled=True),
        lax.psum_scatter(grad_w_value, "batch", scatter_dimension=1, tiled=True),
        lax.psum_scatter(grad_w_output, "batch", scatter_dimension=1, tiled=True),
        lax.psum_scatter(grad_w_in, "batch", scatter_dimension=1, tiled=True),
        lax.psum_scatter(grad_w_out, "batch", scatter_dimension=1, tiled=True),
        lax.psum_scatter(grad_proj, "batch", scatter_dimension=1, tiled=True),
    )
    summed = (
        lax.psum_scatter(
            partial_mats[0].astype(jnp.bfloat16), "seq", scatter_dimension=0, tiled=True
        ).astype(jnp.float32),
        lax.psum_scatter(
            partial_mats[1].astype(jnp.bfloat16), "seq", scatter_dimension=0, tiled=True
        ).astype(jnp.float32),
        lax.psum_scatter(
            partial_mats[2].astype(jnp.bfloat16), "seq", scatter_dimension=0, tiled=True
        ).astype(jnp.float32),
        lax.psum_scatter(
            partial_mats[3].astype(jnp.bfloat16), "seq", scatter_dimension=0, tiled=True
        ).astype(jnp.float32),
        lax.psum_scatter(
            partial_mats[4].astype(jnp.bfloat16), "seq", scatter_dimension=0, tiled=True
        ).astype(jnp.float32),
        lax.psum_scatter(
            partial_mats[5].astype(jnp.bfloat16), "seq", scatter_dimension=0, tiled=True
        ).astype(jnp.float32),
        lax.psum_scatter(
            partial_mats[6].astype(jnp.bfloat16), "seq", scatter_dimension=0, tiled=True
        ).astype(jnp.float32),
    )
    small_sums = lax.psum((grad_gain_one, grad_gain_two, grad_gain_fin, grad_rel), ("batch", "seq"))
    return (
        block_out.reshape(row_count, shard_len, model_dim),
        embedded,
        sent_loss,
        grad_tokens.reshape(row_count, shard_len, model_dim),
        small_sums[0],
        summed[0],
        summed[1],
        summed[2],
        small_sums[3],
        summed[3],
        small_sums[1],
        summed[4],
        summed[5],
        small_sums[2],
        summed[6],
    )


def solution(mesh):
    placed = (
        P("batch", "seq", None),
        P(),
        P(),
        P(),
        P(),
        P(),
        P(),
        P(),
        P(),
        P(),
        P(),
        P(),
        P("batch", None),
        P("batch"),
        P("batch", "seq", None),
    )
    return jax.shard_map(
        shards,
        mesh=mesh,
        in_specs=placed,
        out_specs=(
            P("batch", "seq", None),
            P("batch", None),
            P("batch"),
            P("batch", "seq", None),
            P(),
            P("seq", "batch"),
            P("seq", "batch"),
            P("seq", "batch"),
            P(),
            P("seq", "batch"),
            P(),
            P("seq", "batch"),
            P("seq", "batch"),
            P(),
            P("seq", "batch"),
        ),
        check_vma=False,
    )
```

profile of v0, /device:TPU:0, one launch (start us, length us, event | category | flops | bytes accessed | tf_op | source)
XLA Modules:
  0.0 1075.9 jit_solution(8889892958782430636)
XLA Ops:
  45.5 13.8 %copy.101 = f32[12,256,768]{2,1,0:T(8,128)} copy(f32[12,256,768]{2,0,1:T(8,128)} %fusion.77) | data formatting | bytes 18874368 | tf_op jit(solution)/shard_map/while | solution.py:169
  60.8 29.8 %collective-permute-done.1 = bf16[2,4,256,768]{3,2,1,0:T(8,128)(2,1)} collective-permute-done((bf16[2,4,256,768]{3,2,1,0:T(8,128)(2,1)}, bf16[2,4,256,768]{3,2,1,0:T(8,128)(2,1)}, u32[]{:S(2)}, u32[]{:S(2)}) %collective-permute-start.1) | collective-permute-done | bytes 3145760 | tf_op jit(solution)/shard_map/ppermute | solution.py:21
  122.3 79.0 %while.28 = (s32[]{:T(128)}, bf16[2,2,256,12,64]{2,1,0,4,3:T(2,128)(2,1)}, f32[2,2,12,256,1]{3,2,1,4,0:T(8,128)S(1)}, bf16[2,2,768,12,64]{2,4,3,1,0:T(8,128)(2,1...) while((s32[]{:T(128)}, ...), condition=%wide.region_7.8_spmd, body=%wide.region_4.7_spmd.sunk | while | flops 1264969728 | bytes 94987376 | solution.py:169
  123.3 11.3 %fusion.198 = (f32[2,12,256]{2,1,0:T(8,128)S(1)}, f32[2,12,256,768]{3,2,1,0:T(8,128)}) fusion(f32[12,256,768]{2,1,0:T(8,128)} %get-tuple-element.543, pred[2,256,768]{2,1,0:T(8,128)(4,1)S(1)} %dynamic-slice_bitcast_fusion.6, bf16[2,2,768,12,64]{2,4,3,1,0:T(8,128)(2,1)} %get-tuple-element.542, s32[]{:T(128)S(6)} %copy.160, ...), kind=kOutput, calls=%fused_computation.3.clone.1 | convolution fusion | flops 618129408 | bytes 31876096 | tf_op jit(solution)/shard_map/while/body/eval_jaxpr/bihe,bjhe->bhij/dot_general | solution.py:61
  145.5 13.5 %fusion.200 = bf16[1,2,256,12,64]{2,4,3,1,0:T(8,128)(2,1)} fusion(f32[2,12,256,768]{3,2,1,0:T(8,128)} %get-tuple-element.500, f32[2,12,256]{2,1,0:T(8,128)S(1)} %fusion.199, f32[2,12,256]{2,1,0:T(8,128)S(1)} %get-tuple-element.501, f32[12,256,768]{2,1,0:T(8,128)} %get-tuple-element.543, pred[2,256,768]{2,1,0:T(8,128)(4,1)S(1)} %dynamic-slice_bitcast_fusion.6, ...), kind=kOutput, calls=%fused_computation.13.clone.1 | convolution fusion | flops 627965952 | bytes 31899652 | tf_op jit(solution)/shard_map/while/body/eval_jaxpr/bhij,bjhe->bihe/dot_general | solution.py:71
  162.8 11.3 %fusion.198 = (f32[2,12,256]{2,1,0:T(8,128)S(1)}, f32[2,12,256,768]{3,2,1,0:T(8,128)}) fusion(f32[12,256,768]{2,1,0:T(8,128)} %get-tuple-element.543, pred[2,256,768]{2,1,0:T(8,128)(4,1)S(1)} %dynamic-slice_bitcast_fusion.6, bf16[2,2,768,12,64]{2,4,3,1,0:T(8,128)(2,1)} %get-tuple-element.542, s32[]{:T(128)S(6)} %copy.160, ...), kind=kOutput, calls=%fused_computation.3.clone.1 | convolution fusion | flops 618129408 | bytes 31876096 | tf_op jit(solution)/shard_map/while/body/eval_jaxpr/bihe,bjhe->bhij/dot_general | solution.py:61
  185.0 13.5 %fusion.200 = bf16[1,2,256,12,64]{2,4,3,1,0:T(8,128)(2,1)} fusion(f32[2,12,256,768]{3,2,1,0:T(8,128)} %get-tuple-element.500, f32[2,12,256]{2,1,0:T(8,128)S(1)} %fusion.199, f32[2,12,256]{2,1,0:T(8,128)S(1)} %get-tuple-element.501, f32[12,256,768]{2,1,0:T(8,128)} %get-tuple-element.543, pred[2,256,768]{2,1,0:T(8,128)(4,1)S(1)} %dynamic-slice_bitcast_fusion.6, ...), kind=kOutput, calls=%fused_computation.13.clone.1 | convolution fusion | flops 627965952 | bytes 31899652 | tf_op jit(solution)/shard_map/while/body/eval_jaxpr/bhij,bjhe->bihe/dot_general | solution.py:71
  226.6 38.8 %all-reduce.3.cloned.1.call-done = f32[4,16,768]{2,1,0:T(8,128)} async-done(((f32[4,16,768]{2,1,0:T(8,128)}), f32[4,16,768]{2,1,0:T(8,128)}) %all-reduce.3.cloned.1.call-update) | async-done | bytes 196624 | tf_op jit(solution)/shard_map/psum | solution.py:191
  269.5 25.5 %all-gather.2.cloned.1.call-done = f32[512,768]{1,0:T(8,128)} async-done(((f32[64,768]{1,0:T(8,128)}), f32[512,768]{1,0:T(8,128)}) %all-gather.2.cloned.1.call-update) | async-done | bytes 1572880 | tf_op jit(solution)/shard_map/all_gather | solution.py:199
  302.8 38.3 %reduce-scatter.26.cloned.1.call-done = f32[64,768]{1,0:T(8,128)} async-done(((f32[512,768]{1,0:T(8,128)}), f32[64,768]{1,0:T(8,128)}) %reduce-scatter.26.cloned.1.call-update) | async-done | bytes 196624 | tf_op jit(solution)/shard_map/reduce_scatter | solution.py:215
  355.2 17.1 %fusion.70 = bf16[1024,3072]{1,0:T(8,128)(2,1)} fusion(f32[1024,3072]{1,0:T(8,128)} %copy-done.53, bf16[3072,768]{1,0:T(8,128)(2,1)S(1)} %bitcast.252, f32[1024,768]{1,0:T(8,128)S(1)} %fusion.83), kind=kOutput, calls=%fused_computation.76 | convolution fusion | flops 4895539200 | bytes 26738688 | tf_op jit(solution)/shard_map/td,fd->tf/dot_general | solution.py:233
  401.0 169.2 %while.29 = (s32[]{:T(128)}, bf16[2,2,256,12,64]{2,1,0,4,3:T(2,128)(2,1)}, f32[2,2,768,12,64]{2,4,3,1,0:T(8,128)}, f32[2,2,768,12,64]{2,4,3,1,0:T(8,128)}, f32[2...) while((s32[]{:T(128)}, ...), condition=%wide.region_22.23_spmd, body=%wide.region_19.22_spmd.sunk | while | flops 3093424128 | bytes 263235920 | solution.py:254
  405.5 11.2 %fusion.208 = f32[2,12,256,768]{3,2,1,0:T(8,128)} fusion(bf16[2,2,768,12,64]{2,4,3,1,0:T(8,128)(2,1)} %get-tuple-element.576, s32[]{:T(128)S(6)} %copy.172, bf16[2,2,256,12,64]{2,4,3,1,0:T(8,128)(2,1)} %copy-done.1), kind=kOutput, calls=%fused_computation.40.clone.1 | convolution fusion | flops 603979776 | bytes 22021120 | tf_op jit(solution)/shard_map/while/body/eval_jaxpr/bihe,bjhe->bhij/dot_general | solution.py:61
  416.8 14.2 %bitcast_dynamic-update-slice_fusion.10 = f32[2,2,768,12,64]{2,4,3,1,0:T(8,128)} fusion(f32[2,2,768,12,64]{2,4,3,1,0:T(8,128)} %get-tuple-element.561, s32[]{:T(128)S(6)} %copy.172, f32[2,12,256,768]{3,2,1,0:T(8,128)} %fusion.208, f32[2,12,256]{2,1,0:T(8,128)S(1)} %dynamic-slice_bitcast_fusion.7, f32[12,256,768]{2,1,0:T(8,128)} %get-tuple-element.579, ...), kind=kOutput, calls=%fused_computation.31.clone.1 | convolution fusion | flops 622854144 | bytes 34234372 | tf_op jit(solution)/shard_map/while/body/eval_jaxpr/bhij,bihe->bjhe/dot_general | solution.py:90
  431.0 17.2 %multiply_reduce_fusion.7 = (f32[2,12,256]{2,1,0:T(8,128)S(1)}, f32[2,12,256,768]{3,2,1,0:T(8,128)}) fusion(f32[2,12,256,768]{3,2,1,0:T(8,128)} %fusion.208, f32[2,12,256]{2,1,0:T(8,128)S(1)} %dynamic-slice_bitcast_fusion.7, f32[12,256,768]{2,1,0:T(8,128)} %get-tuple-element.579, pred[2,256,768]{2,1,0:T(8,128)(4,1)S(1)} %dynamic-slice_bitcast_fusion.8, ...), kind=kOutput, calls=%fused_computation.22.clone.1 | convolution fusion | flops 627566592 | bytes 50774020 | tf_op jit(solution)/shard_map/while/body/eval_jaxpr/bihe,bjhe->bhij/dot_general | solution.py:80
  448.2 20.2 %fusion.209 = (f32[12,256,768]{2,1,0:T(8,128)}, bf16[2,12,256,768]{3,2,1,0:T(8,128)(2,1)S(1)}) fusion(f32[2,12,256,768]{3,2,1,0:T(8,128)} %get-tuple-element.514, f32[2,12,256]{2,1,0:T(8,128)S(1)} %get-tuple-element.515, f32[2,12,256]{2,1,0:T(8,128)S(1)} %dynamic-slice_bitcast_fusion.7, f32[2,12,256,768]{3,2,1,0:T(8,128)} %fusion.208, ...), kind=kLoop, calls=%fused_computation.197.clone.1 | loop fusion | flops 30670848 | bytes 66502656 | tf_op jit(solution)/shard_map/while/body/eval_jaxpr/reduce_sum | solution.py:96
  490.2 11.0 %fusion.208 = f32[2,12,256,768]{3,2,1,0:T(8,128)} fusion(bf16[2,2,768,12,64]{2,4,3,1,0:T(8,128)(2,1)} %get-tuple-element.576, s32[]{:T(128)S(6)} %copy.172, bf16[2,2,256,12,64]{2,4,3,1,0:T(8,128)(2,1)} %copy-done.1), kind=kOutput, calls=%fused_computation.40.clone.1 | convolution fusion | flops 603979776 | bytes 22021120 | tf_op jit(solution)/shard_map/while/body/eval_jaxpr/bihe,bjhe->bhij/dot_general | solution.py:61
  501.2 13.8 %bitcast_dynamic-update-slice_fusion.10 = f32[2,2,768,12,64]{2,4,3,1,0:T(8,128)} fusion(f32[2,2,768,12,64]{2,4,3,1,0:T(8,128)} %get-tuple-element.561, s32[]{:T(128)S(6)} %copy.172, f32[2,12,256,768]{3,2,1,0:T(8,128)} %fusion.208, f32[2,12,256]{2,1,0:T(8,128)S(1)} %dynamic-slice_bitcast_fusion.7, f32[12,256,768]{2,1,0:T(8,128)} %get-tuple-element.579, ...), kind=kOutput, calls=%fused_computation.31.clone.1 | convolution fusion | flops 622854144 | bytes 34234372 | tf_op jit(solution)/shard_map/while/body/eval_jaxpr/bhij,bihe->bjhe/dot_general | solution.py:90
  515.1 17.0 %multiply_reduce_fusion.7 = (f32[2,12,256]{2,1,0:T(8,128)S(1)}, f32[2,12,256,768]{3,2,1,0:T(8,128)}) fusion(f32[2,12,256,768]{3,2,1,0:T(8,128)} %fusion.208, f32[2,12,256]{2,1,0:T(8,128)S(1)} %dynamic-slice_bitcast_fusion.7, f32[12,256,768]{2,1,0:T(8,128)} %get-tuple-element.579, pred[2,256,768]{2,1,0:T(8,128)(4,1)S(1)} %dynamic-slice_bitcast_fusion.8, ...), kind=kOutput, calls=%fused_computation.22.clone.1 | convolution fusion | flops 627566592 | bytes 50774020 | tf_op jit(solution)/shard_map/while/body/eval_jaxpr/bihe,bjhe->bhij/dot_general | solution.py:80
  532.1 20.2 %fusion.209 = (f32[12,256,768]{2,1,0:T(8,128)}, bf16[2,12,256,768]{3,2,1,0:T(8,128)(2,1)S(1)}) fusion(f32[2,12,256,768]{3,2,1,0:T(8,128)} %get-tuple-element.514, f32[2,12,256]{2,1,0:T(8,128)S(1)} %get-tuple-element.515, f32[2,12,256]{2,1,0:T(8,128)S(1)} %dynamic-slice_bitcast_fusion.7, f32[2,12,256,768]{3,2,1,0:T(8,128)} %fusion.208, ...), kind=kLoop, calls=%fused_computation.197.clone.1 | loop fusion | flops 30670848 | bytes 66502656 | tf_op jit(solution)/shard_map/while/body/eval_jaxpr/reduce_sum | solution.py:96
  598.4 54.2 %collective-permute-done.2 = bf16[2,4,256,768]{2,3,1,0:T(8,128)(2,1)} collective-permute-done((bf16[2,4,256,768]{2,3,1,0:T(8,128)(2,1)}, bf16[2,4,256,768]{2,3,1,0:T(8,128)(2,1)}, u32[]{:S(2)}, u32[]{:S(2)}) %collective-permute-start.2) | collective-permute-done | bytes 3145760 | tf_op jit(solution)/shard_map/ppermute | solution.py:29
  675.7 12.1 %fusion.109 = f32[3072,768]{0,1:T(8,128)} fusion(f32[1024,768]{1,0:T(8,128)} %copy-done.6, f32[1024,3072]{1,0:T(8,128)} %copy-done.53), kind=kOutput, calls=%fused_computation.145 | convolution fusion | flops 4860936192 | bytes 25165824 | tf_op jit(solution)/shard_map/tf,td->fd/dot_general | solution.py:232
  715.9 44.4 %reduce-scatter.32.cloned.1.call-done = f32[768,96]{0,1:T(8,128)} async-done(((f32[768,768]{0,1:T(8,128)}), f32[768,96]{0,1:T(8,128)}) %reduce-scatter.32.cloned.1.call-update) | async-done | bytes 294928 | tf_op jit(solution)/shard_map/reduce_scatter | solution.py:295
  762.6 77.6 %reduce-scatter.40.cloned.1.call-done = f32[3072,96]{0,1:T(8,128)} async-done(((f32[3072,768]{0,1:T(8,128)}), f32[3072,96]{0,1:T(8,128)}) %reduce-scatter.40.cloned.1.call-update) | async-done | bytes 1179664 | tf_op jit(solution)/shard_map/reduce_scatter | solution.py:298
  847.3 15.0 %reduce_sum.184 = f32[12,256,768]{2,1,0:T(8,128)} reduce(f32[2,12,256,768]{3,2,1,0:T(8,128)} %get-tuple-element.128, f32[]{:T(128)} %constant.49.clone.1), dimensions={0}, to_apply=%region_32.33 | reduce | flops 2359296 | bytes 28311556 | tf_op jit(solution)/shard_map/reduce_sum | solution.py:258
  862.4 18.8 %fusion.102 = f32[32,12]{0,1:T(8,128)S(1)} fusion(f32[12,256,768]{2,1,0:T(8,128)} %reduce_sum.184, s32[256,768]{1,0:T(8,128)S(1)} %copy-done.9), kind=kOutput, calls=%fused_computation.140 | convolution fusion | flops 912261120 | bytes 10225152 | tf_op jit(solution)/shard_map/hij,ijc->ch/dot_general | solution.py:257
  884.3 35.8 %reduce-scatter.36.cloned.1.call-done = f32[768,384]{1,0:T(8,128)} async-done(((f32[768,3072]{1,0:T(8,128)}), f32[768,384]{1,0:T(8,128)}) %reduce-scatter.36.cloned.1.call-update) | async-done | bytes 1179664 | tf_op jit(solution)/shard_map/reduce_scatter | solution.py:297
  929.2 40.0 %all-reduce = (f32[768]{0:T(1024)}, f32[32,12]{0,1:T(8,128)}, f32[768]{0:T(1024)}, f32[768]{0:T(1024)}) all-reduce(f32[768]{0:T(1024)S(1)} %get-tuple-element.308, f32[32,12]{0,1:T(8,128)S(1)} %fusion.102, f32[768]{0:T(1024)S(1)} %copy-done.45, f32[768]{0:T(1024)S(1)} %copy-done.35), channel_id=1, replica_groups=mesh['batch'=8,'seq'=4] {'batch','seq'}, use_global_device_ids=true, to_apply=%region_25.26 | all-reduce | flops 2688 | bytes 21504 | tf_op jit(solution)/shard_map/psum | solution.py:324
  984.0 18.8 %reduce-scatter.48.cloned.1.call-done = bf16[192,96]{1,0:T(8,128)(2,1)} async-done(((bf16[768,96]{1,0:T(8,128)(2,1)}), bf16[192,96]{1,0:T(8,128)(2,1)}) %reduce-scatter.48.cloned.1.call-update) | async-done | bytes 36880
  1004.4 18.1 %reduce-scatter.50.cloned.1.call-done = bf16[192,96]{1,0:T(8,128)(2,1)} async-done(((bf16[768,96]{1,0:T(8,128)(2,1)}), bf16[192,96]{1,0:T(8,128)(2,1)}) %reduce-scatter.50.cloned.1.call-update) | async-done | bytes 36880
  1024.1 20.8 %reduce-scatter.42.cloned.1.call-done = bf16[768,96]{0,1:T(8,128)(2,1)} async-done(((bf16[3072,96]{0,1:T(8,128)(2,1)}), bf16[768,96]{0,1:T(8,128)(2,1)}) %reduce-scatter.42.cloned.1.call-update) | async-done | bytes 147472 | tf_op jit(solution)/shard_map/reduce_scatter | solution.py:317
  1046.5 21.0 %reduce-scatter.38.cloned.1.call-done = bf16[192,384]{1,0:T(8,128)(2,1)} async-done(((bf16[768,384]{1,0:T(8,128)(2,1)}), bf16[192,384]{1,0:T(8,128)(2,1)}) %reduce-scatter.38.cloned.1.call-update) | async-done | bytes 147472 | tf_op jit(solution)/shard_map/reduce_scatter | solution.py:314
  (314 shorter events, 345.5 us)
Async XLA Ops:
  7.2 258.3 %all-reduce.3.cloned.1.call-start = ((), (), s32[]{:S(2)}) async-start(), calls=%async_computation.15 | async-start | bytes 393216 | tf_op jit(solution)/shard_map/psum | solution.py:191
  17.3 73.3 %collective-permute-start.1 = (bf16[2,4,256,768]{3,2,1,0:T(8,128)(2,1)}, bf16[2,4,256,768]{3,2,1,0:T(8,128)(2,1)}, u32[]{:S(2)}, u32[]{:S(2)}) collective-permute-start(bf16[2,4,256,768]{3,2,1,0:T(8,128)(2,1)} %pad_maximum_fusion.2), channel_id=1, source_target_pairs={{1,0},{2,1},{3,2},{5,4},{6,5},{7,6},{9,8},{10,9},{11,10},{13,12},{... | collective-permute-start | bytes 9437192 | tf_op jit(solution)/shard_map/ppermute | solution.py:21
  18.6 73.2 %collective-permute-start = (bf16[2,4,256,768]{3,2,1,0:T(8,128)(2,1)}, bf16[2,4,256,768]{3,2,1,0:T(8,128)(2,1)}, u32[]{:S(2)}, u32[]{:S(2)}) collective-permute-start(bf16[2,4,256,768]{3,2,1,0:T(8,128)(2,1)} %pad_maximum_fusion.2), channel_id=1, source_target_pairs={{0,1},{1,2},{2,3},{4,5},{5,6},{6,7},{8,9},{9,10},{10,11},{12,13},{... | collective-permute-start | bytes 9437192 | tf_op jit(solution)/shard_map/ppermute | solution.py:18
  45.5 46.3 %copy-start.12 = (bf16[1024,768]{1,0:T(8,128)(2,1)S(1)}, bf16[1024,768]{1,0:T(8,128)(2,1)}, u32[]{:S(2)}) copy-start(bf16[1024,768]{1,0:T(8,128)(2,1)} %copy-done.11) | copy-start | bytes 4718596
  45.5 46.3 %copy-start.14 = (bf16[1024,768]{1,0:T(8,128)(2,1)S(1)}, bf16[1024,768]{1,0:T(8,128)(2,1)}, u32[]{:S(2)}) copy-start(bf16[1024,768]{1,0:T(8,128)(2,1)} %copy-done.13) | copy-start | bytes 4718596
  226.5 71.7 %copy-start.43 = (s32[64]{0:T(128)S(1)}, s32[64]{0:T(128)}, u32[]{:S(2)}) copy-start(s32[64]{0:T(128)} %param.32) | copy-start | bytes 772
  226.6 68.4 %all-gather.2.cloned.1.call-start = ((), (), s32[]{:S(2)}) async-start(), calls=%async_computation.16 | async-start | bytes 1769472 | tf_op jit(solution)/shard_map/all_gather | solution.py:199
  269.4 71.8 %copy-start.10 = (f32[64,768]{1,0:T(8,128)S(1)}, f32[64,768]{1,0:T(8,128)}, u32[]{:S(2)}) copy-start(f32[64,768]{1,0:T(8,128)} %broadcast_multiply_fusion) | copy-start | bytes 589828
  269.4 71.8 %reduce-scatter.26.cloned.1.call-start = ((), (), s32[]{:S(2)}) async-start(), calls=%async_computation.17 | async-start | bytes 1769472 | tf_op jit(solution)/shard_map/reduce_scatter | solution.py:215
  298.2 45.6 %copy-start.36 = (f32[64]{0:T(128)}, f32[64]{0:T(128)S(1)}, u32[]{:S(2)}) copy-start(f32[64]{0:T(128)S(1)} %get-tuple-element.376) | copy-start | bytes 772
  298.9 44.9 %copy-start.40 = (f32[64]{0:T(128)}, f32[64]{0:T(128)S(1)}, u32[]{:S(2)}) copy-start(f32[64]{0:T(128)S(1)} %get-tuple-element.310) | copy-start | bytes 772
  302.5 396.6 %reduce-scatter.44.cloned.1.call-start = ((), (), s32[]{:S(2)}) async-start(), calls=%async_computation.26 | async-start | bytes 2654208 | tf_op jit(solution)/shard_map/reduce_scatter | solution.py:299
  350.5 350.5 %reduce-scatter.34.cloned.1.call-start = ((), (), s32[]{:S(2)}) async-start(), calls=%async_computation.21 | async-start | bytes 2654208 | tf_op jit(solution)/shard_map/reduce_scatter | solution.py:296
  398.7 304.3 %reduce-scatter.28.cloned.1.call-start = ((), (), s32[]{:S(2)}) async-start(), calls=%async_computation.18 | async-start | bytes 2654208 | tf_op jit(solution)/shard_map/reduce_scatter | solution.py:293
  431.0 37.4 %slice-start = ((s8[4718592]{0:T(1024)(128)(4,1)}), s8[524288]{0:T(1024)(128)(4,1)S(1)}, s32[]{:S(2)}) async-start(s8[4718592]{0:T(1024)(128)(4,1)} %bitcast.222), calls=%async_computation.32 | async-start | bytes 1048576 | tf_op jit(solution)/shard_map/while
  580.7 71.9 %collective-permute-start.2 = (bf16[2,4,256,768]{2,3,1,0:T(8,128)(2,1)}, bf16[2,4,256,768]{2,3,1,0:T(8,128)(2,1)}, u32[]{:S(2)}, u32[]{:S(2)}) collective-permute-start(bf16[2,4,256,768]{2,3,1,0:T(8,128)(2,1)} %get-tuple-element.362), channel_id=1, source_target_pairs={{1,0},{2,1},{3,2},{5,4},{6,5},{7,6},{9,8},{10,9},{11,10},{13,12},{... | collective-permute-start | bytes 9437192 | tf_op jit(solution)/shard_map/ppermute | solution.py:29
  582.0 71.8 %collective-permute-start.3 = (bf16[2,4,256,768]{2,3,1,0:T(8,128)(2,1)}, bf16[2,4,256,768]{2,3,1,0:T(8,128)(2,1)}, u32[]{:S(2)}, u32[]{:S(2)}) collective-permute-start(bf16[2,4,256,768]{2,3,1,0:T(8,128)(2,1)} %get-tuple-element.363), channel_id=1, source_target_pairs={{0,1},{1,2},{2,3},{4,5},{5,6},{6,7},{8,9},{9,10},{10,11},{12,13},{... | collective-permute-start | bytes 9437192 | tf_op jit(solution)/shard_map/ppermute | solution.py:29
  598.3 115.6 %reduce-scatter.30.cloned.1.call-start = ((), (), s32[]{:S(2)}) async-start(), calls=%async_computation.19 | async-start | bytes 2654208 | tf_op jit(solution)/shard_map/reduce_scatter | solution.py:294
  668.2 92.0 %reduce-scatter.32.cloned.1.call-start = ((), (), s32[]{:S(2)}) async-start(), calls=%async_computation.20 | async-start | bytes 2654208 | tf_op jit(solution)/shard_map/reduce_scatter | solution.py:295
  675.7 164.6 %reduce-scatter.40.cloned.1.call-start = ((), (), s32[]{:S(2)}) async-start(), calls=%async_computation.24 | async-start | bytes 10616832 | tf_op jit(solution)/shard_map/reduce_scatter | solution.py:298
  687.8 232.3 %reduce-scatter.36.cloned.1.call-start = ((), (), s32[]{:S(2)}) async-start(), calls=%async_computation.22 | async-start | bytes 10616832 | tf_op jit(solution)/shard_map/reduce_scatter | solution.py:297
  699.1 63.0 %copy-start.37 = (f32[64]{0:T(128)S(1)}, f32[64]{0:T(128)}, u32[]{:S(2)}) copy-start(f32[64]{0:T(128)} %copy-done.36) | copy-start | bytes 772
  699.1 63.0 %copy-start.41 = (f32[64]{0:T(128)S(1)}, f32[64]{0:T(128)}, u32[]{:S(2)}) copy-start(f32[64]{0:T(128)} %copy-done.40) | copy-start | bytes 772
  699.1 63.0 %copy-start.46 = (f32[64]{0:T(128)S(1)}, f32[64]{0:T(128)}, u32[]{:S(2)}) copy-start(f32[64]{0:T(128)} %get-tuple-element.311) | copy-start | bytes 772
  699.1 275.5 %reduce-scatter.54.cloned.1.call-start = ((), (), s32[]{:S(2)}) async-start(), calls=%async_computation.31 | async-start | bytes 245760
  701.0 275.3 %reduce-scatter.52.cloned.1.call-start = ((), (), s32[]{:S(2)}) async-start(), calls=%async_computation.30 | async-start | bytes 245760
  702.9 279.5 %reduce-scatter.46.cloned.1.call-start = ((), (), s32[]{:S(2)}) async-start(), calls=%async_computation.27 | async-start | bytes 245760
  704.8 298.0 %reduce-scatter.48.cloned.1.call-start = ((), (), s32[]{:S(2)}) async-start(), calls=%async_computation.28 | async-start | bytes 245760
  715.8 306.7 %reduce-scatter.50.cloned.1.call-start = ((), (), s32[]{:S(2)}) async-start(), calls=%async_computation.29 | async-start | bytes 245760
  762.0 282.8 %reduce-scatter.42.cloned.1.call-start = ((), (), s32[]{:S(2)}) async-start(), calls=%async_computation.25 | async-start | bytes 737280 | tf_op jit(solution)/shard_map/reduce_scatter | solution.py:317
  842.4 225.1 %reduce-scatter.38.cloned.1.call-start = ((), (), s32[]{:S(2)}) async-start(), calls=%async_computation.23 | async-start | bytes 737280 | tf_op jit(solution)/shard_map/reduce_scatter | solution.py:314
  881.2 41.1 %copy-start.25 = (f32[1,2,4,128]{3,1,2,0:T(2,128)S(1)}, f32[1,2,4,128]{3,1,2,0:T(2,128)}, u32[]{:S(2)}) copy-start(f32[1,2,4,128]{3,1,2,0:T(2,128)} %copy-done.24) | copy-start | bytes 12292
  (55 other events, 434.2 us)
Sparse Core Ops, SparseCore 0:
  226.7 38.7 all-reduce.2
  269.5 25.3 all-gather.1
  302.7 38.4 reduce-scatter.25
  350.7 42.4 reduce-scatter.43
  398.8 42.7 reduce-scatter.33
  598.5 41.7 reduce-scatter.27
  668.3 45.5 reduce-scatter.29
  717.7 42.4 reduce-scatter.31
  763.7 76.4 reduce-scatter.39
  843.6 76.4 reduce-scatter.35
  922.4 19.3 reduce-scatter.53
  944.0 17.6 reduce-scatter.51
  964.5 17.8 reduce-scatter.45
  985.1 17.5 reduce-scatter.47
  1004.9 17.5 reduce-scatter.49
  1024.7 20.1 reduce-scatter.41
  1047.1 20.3 reduce-scatter.37
where the time goes:
time: 1080 us
  waiting for transfers between devices  439 us (41%)
  matrix products  308 us (29%)
  other arithmetic  134 us (12%)
  local copies, waits for them, and re-layouts  122 us (11%)
  blocking collectives  40 us (4%)
  starting transfers between devices  16.9 us (2%)
  between operations  15.1 us (1%)
    reduce_scatter x1, waiting for transfers between devices, shards(): lax.psum_scatter(grad_w_out, 'batch', scatter_dimension=1, tiled=True)  77.6 us
    ppermute x2, waiting for transfers between devices, shifted(): return lax.ppermute(block, axis, route)  55.4 us
    dot_general x4, matrix products, scores_of(): jnp.einsum('bihe,bjhe->bhij', block_q, block_k, preferred_element_type=jn...  45 us
    reduce_scatter x1, waiting for transfers between devices, shards(): lax.psum_scatter(grad_w_value, 'batch', scatter_dimension=1, tiled=True)  44.4 us
    unnamed x22, waiting for transfers between devices  41.6 us
    reduce_sum x2, other arithmetic, attend_back(): jnp.sum(grad_scores, axis=0)  40.4 us
    psum x1, blocking collectives, shards(): lax.psum((grad_gain_one, grad_gain_two, grad_gain_fin, grad_rel), ('batch...  40 us
    psum x1, waiting for transfers between devices, shards(): pooled_sum = lax.psum(partial_sums, 'seq')  38.8 us
  transfers between devices with their start and end apart: 21, of which 16 were waited for; matrix products, arithmetic and copies ran while one was open for 36% of the time, Pallas kernels for 0%

commit v1 on v0

v1 whole, which is shorter than its diff:
```python
import functools

import jax
import jax.numpy as jnp
from jax import lax
from jax.experimental import pallas as pl
from jax.experimental.pallas import tpu as pltpu
from jax.sharding import PartitionSpec as P

EPS = 1e-06
NEGATIVE = -1e30
SHARPNESS = 50.0
THRESHOLDS = (12, 16, 23, 32, 46, 64, 91)
HIGHEST = lax.Precision.HIGHEST
BF = jnp.bfloat16
F32 = jnp.float32
VMEM_BYTES = 60 * 1024 * 1024
GELU_A = 0.7978845608028654
GELU_B = 0.044715


def dot_nn(left, right):
    return lax.dot_general(left, right, (((1,), (0,)), ((), ())), preferred_element_type=F32)


def dot_nt(left, right):
    return lax.dot_general(left, right, (((1,), (1,)), ((), ())), preferred_element_type=F32)


def dot_tn(left, right):
    return lax.dot_general(left, right, (((0,), (0,)), ((), ())), preferred_element_type=F32)


def rms_scale(values):
    return lax.rsqrt(jnp.mean(values * values, axis=-1, keepdims=True) + EPS)


def rms_back(values, scale, grad_normed):
    inner = jnp.mean(grad_normed * values, axis=-1, keepdims=True)
    return scale * (grad_normed - values * (scale * scale * inner))


def split_bf(values):
    high = values.astype(BF)
    return high, (values - high.astype(F32)).astype(BF)


def bucket_of(offset):
    distance = jnp.abs(offset)
    beyond = jnp.zeros_like(distance)
    for threshold in THRESHOLDS:
        beyond = beyond + (distance >= threshold).astype(jnp.int32)
    within = jnp.where(distance < 8, distance, 8 + beyond)
    return within + 16 * (offset > 0).astype(jnp.int32)


def wrapped_offsets(shape, axis, size):
    place = lax.broadcasted_iota(jnp.int32, shape, axis)
    return jnp.where(place < size, place, place - 2 * size)


def full(shape):
    return pl.BlockSpec(shape, lambda *_: (0,) * len(shape), pipeline_mode=pl.Buffered(1))


def row_spec(shape, first=0):
    return pl.BlockSpec(
        (1,) + tuple(shape), lambda step, *_: (step + first,) + (0,) * len(shape)
    )


def params(limit=VMEM_BYTES):
    return pltpu.CompilerParams(
        vmem_limit_bytes=limit, dimension_semantics=("arbitrary",)
    )


def bias_kernel(size, table_ref, out_ref):
    buckets, heads = table_ref.shape
    hot = (
        lax.broadcasted_iota(jnp.int32, (buckets, 2 * size), 0)
        == bucket_of(wrapped_offsets((buckets, 2 * size), 1, size))
    ).astype(BF)
    by_offset = dot_tn(table_ref[...], hot)
    for head in range(heads):
        line = jnp.broadcast_to(by_offset[head : head + 1, :], (size, 2 * size))
        out_ref[head] = pltpu.roll(line, 0, 1, stride=1, stride_axis=0).astype(BF)


def bias_tables(rel_bias, size):
    heads = rel_bias.shape[1]
    return pl.pallas_call(
        functools.partial(bias_kernel, size),
        out_shape=jax.ShapeDtypeStruct((heads, size, 2 * size), BF),
        compiler_params=pltpu.CompilerParams(vmem_limit_bytes=VMEM_BYTES),
    )(rel_bias)


def bias_grad_kernel(acc_ref, out_ref):
    heads, size, width = acc_ref.shape
    buckets = out_ref.shape[0]
    hot = (
        lax.broadcasted_iota(jnp.int32, (width, buckets), 1)
        == bucket_of(wrapped_offsets((width, buckets), 0, size))
    ).astype(F32)
    lines = []
    for head in range(heads):
        rows = acc_ref[head]
        count = size
        while count > 1:
            count = count // 2
            rows = rows[:count] + pltpu.roll(rows[count:], width - count, 1)
        lines.append(rows)
    table = jnp.concatenate(lines, axis=0)
    out_ref[...] = lax.dot_general(
        hot, table, (((0,), (1,)), ((), ())), preferred_element_type=F32, precision=HIGHEST
    )


def bias_grad(acc, buckets):
    return pl.pallas_call(
        bias_grad_kernel,
        out_shape=jax.ShapeDtypeStruct((buckets, acc.shape[0]), F32),
        compiler_params=pltpu.CompilerParams(vmem_limit_bytes=VMEM_BYTES),
    )(acc)


def row_masks(lengths_ref, place_ref, row, size):
    slots = lengths_ref.shape[1]
    base = place_ref[0] * size
    col_pos = base + lax.broadcasted_iota(jnp.int32, (size, 1), 0)
    row_pos = base + lax.broadcasted_iota(jnp.int32, (1, size), 1)
    seg_col = jnp.zeros((size, 1), jnp.int32)
    seg_own = jnp.zeros((1, size), jnp.int32)
    seg_low = jnp.zeros((1, size), jnp.int32)
    seg_high = jnp.zeros((1, size), jnp.int32)
    end = jnp.int32(0)
    for slot in range(slots):
        end = end + lengths_ref[row, slot]
        seg_col = seg_col + (end <= col_pos).astype(jnp.int32)
        seg_own = seg_own + (end <= row_pos).astype(jnp.int32)
        seg_low = seg_low + (end <= row_pos - size).astype(jnp.int32)
        seg_high = seg_high + (end <= row_pos + size).astype(jnp.int32)
    seg_low = jnp.where(row_pos < size, -1, seg_low)
    upper = lax.broadcasted_iota(jnp.int32, (size, size), 1) > lax.broadcasted_iota(
        jnp.int32, (size, size), 0
    )
    own = (seg_col == seg_own).astype(F32)
    above = upper.astype(F32)
    low = (seg_col == seg_low).astype(F32) * above
    high = (seg_col == seg_high).astype(F32) * (1.0 - above)
    return seg_col, seg_own, own, low, high


def forward_kernel(
    first,
    lengths_ref,
    place_ref,
    own_ref,
    low_ref,
    high_ref,
    gain1_ref,
    gain2_ref,
    gainf_ref,
    wq_ref,
    wk_ref,
    wv_ref,
    wo_ref,
    win_ref,
    wout_ref,
    bias_ref,
    block_ref,
    pooled_ref,
    n1_ref,
    q_ref,
    k_ref,
    v_ref,
    p_ref,
    att_ref,
    after_ref,
    n2_ref,
    act_ref,
    dact_ref,
    mask_ref,
):
    size, dim = own_ref.shape[1:]
    heads = bias_ref.shape[0]
    pairs = heads // 2
    lanes = dim // pairs
    hidden = win_ref.shape[1]
    slots = pooled_ref.shape[1]
    row = pl.program_id(0) + first
    seg_col, seg_own, own, low, high = row_masks(lengths_ref, place_ref, row, size)
    mask_ref[0] = own.astype(BF)
    mask_ref[1] = low.astype(BF)
    mask_ref[2] = high.astype(BF)
    gain1 = gain1_ref[...].astype(F32)
    for part, source in enumerate((low_ref, own_ref, high_ref)):
        x = source[0].astype(F32)
        n1_ref[0, part] = (x * rms_scale(x) * gain1).astype(BF)
    q_ref[0] = dot_nn(n1_ref[0, 1], wq_ref[...]).astype(BF)
    for part in range(3):
        k_ref[0, part] = dot_nn(n1_ref[0, part], wk_ref[...]).astype(BF)
        v_ref[0, part] = dot_nn(n1_ref[0, part], wv_ref[...]).astype(BF)
    first_half = lax.broadcasted_iota(jnp.int32, (1, lanes), 1) < lanes // 2
    for pair in range(pairs):
        cols = slice(pair * lanes, (pair + 1) * lanes)
        q_pair = q_ref[0, :, cols]
        halves = []
        for half in range(2):
            head = 2 * pair + half
            keep = first_half if half == 0 else jnp.logical_not(first_half)
            q_head = jnp.where(keep, q_pair, jnp.zeros_like(q_pair))
            own_on = mask_ref[0].astype(F32) > 0
            low_on = mask_ref[1].astype(F32) > 0
            high_on = mask_ref[2].astype(F32) > 0
            s_own = dot_nt(q_head, k_ref[0, 1, :, cols]) + bias_ref[head, :, :size].astype(F32)
            s_low = dot_nt(q_head, k_ref[0, 0, :, cols])
            s_high = dot_nt(q_head, k_ref[0, 2, :, cols])
            s_alt = jnp.where(low_on, s_low, s_high) + bias_ref[head, :, size:].astype(F32)
            scores = jnp.where(
                own_on, s_own, jnp.where(low_on | high_on, s_alt, NEGATIVE)
            )
            peak = jnp.max(scores, axis=-1, keepdims=True)
            powers = jnp.exp(scores - peak)
            inverse = 1.0 / jnp.sum(powers, axis=-1, keepdims=True)
            probs = (powers * inverse).astype(BF)
            p_ref[0, head] = probs
            mixed = dot_nn(probs * mask_ref[1], v_ref[0, 0, :, cols])
            mixed += dot_nn(probs * mask_ref[0], v_ref[0, 1, :, cols])
            mixed += dot_nn(probs * mask_ref[2], v_ref[0, 2, :, cols])
            halves.append(mixed)
        att_ref[0, :, cols] = jnp.where(first_half, halves[0], halves[1]).astype(BF)
    after = own_ref[0].astype(F32) + dot_nn(att_ref[0], wo_ref[...])
    after_ref[0] = after
    n2_ref[0] = (after * rms_scale(after) * gain2_ref[...].astype(F32)).astype(BF)
    total = after
    chunk = dim
    for start in range(0, hidden, chunk):
        cols = slice(start, start + chunk)
        pre = dot_nn(n2_ref[0], win_ref[:, cols])
        square = pre * pre
        gate = 0.5 + 0.5 * jnp.tanh(pre * (GELU_A + (GELU_A * GELU_B) * square))
        act = pre * gate
        slope = gate + act * (1.0 - gate) * (2 * GELU_A + (6 * GELU_A * GELU_B) * square)
        act_ref[0, :, cols] = act.astype(BF)
        dact_ref[0, :, cols] = slope.astype(BF)
        total = total + dot_nn(act_ref[0, :, cols], wout_ref[cols, :])
    block = total.astype(BF)
    block_ref[0] = block
    out = block.astype(F32)
    final = out * rms_scale(out) * gainf_ref[...].astype(F32)
    member = (lax.broadcasted_iota(jnp.int32, (slots, size), 0) == seg_own).astype(BF)
    high_part, low_part = split_bf(final)
    pooled_ref[0] = dot_nn(member, high_part) + dot_nn(member, low_part)


def forward(first, count, lengths, place, own, low, high, gains, weights, bias):
    size, dim = own.shape[1:]
    heads = bias.shape[0]
    slots = lengths.shape[1]
    hidden = weights[4].shape[1]
    outs = (
        ((size, dim), BF),
        ((slots, dim), F32),
        ((3, size, dim), BF),
        ((size, dim), BF),
        ((3, size, dim), BF),
        ((3, size, dim), BF),
        ((heads, size, size), BF),
        ((size, dim), BF),
        ((size, dim), F32),
        ((size, dim), BF),
        ((size, hidden), BF),
        ((size, hidden), BF),
    )
    constants = tuple(gains) + tuple(weights) + (bias,)
    return pl.pallas_call(
        functools.partial(forward_kernel, first),
        grid_spec=pltpu.PrefetchScalarGridSpec(
            num_scalar_prefetch=2,
            grid=(count,),
            in_specs=[row_spec((size, dim), first)]
            + [row_spec((size, dim), 0)] * 2
            + [full(item.shape) for item in constants],
            out_specs=[row_spec(shape) for shape, _ in outs],
            scratch_shapes=[pltpu.VMEM((3, size, size), BF)],
        ),
        out_shape=[jax.ShapeDtypeStruct((count,) + shape, kind) for shape, kind in outs],
        compiler_params=params(),
        name="forward_rows",
    )(lengths, place, own, low, high, *constants)


def feed_back_kernel(
    lengths_ref,
    place_ref,
    block_ref,
    after_ref,
    cot_ref,
    pool_ref,
    dact_ref,
    gain2_ref,
    gainf_ref,
    wo_ref,
    win_ref,
    wout_ref,
    branch_ref,
    pre_ref,
    gafter_ref,
    gmix_ref,
    gains_ref,
):
    size, dim = block_ref.shape[1:]
    hidden = win_ref.shape[1]
    slots = pool_ref.shape[1]
    row = pl.program_id(0)
    base = place_ref[0] * size
    col_pos = base + lax.broadcasted_iota(jnp.int32, (size, 1), 0)
    seg_col = jnp.zeros((size, 1), jnp.int32)
    end = jnp.int32(0)
    for slot in range(slots):
        end = end + lengths_ref[row, slot]
        seg_col = seg_col + (end <= col_pos).astype(jnp.int32)
    member = (lax.broadcasted_iota(jnp.int32, (size, slots), 1) == seg_col).astype(BF)
    high_part, low_part = split_bf(pool_ref[0])
    g_final = dot_nn(member, high_part) + dot_nn(member, low_part)
    out = block_ref[0].astype(F32)
    scale = rms_scale(out)
    gain_f = jnp.sum(g_final * out * scale, axis=0, keepdims=True)
    g_out = rms_back(out, scale, g_final * gainf_ref[...].astype(F32)) + cot_ref[0].astype(F32)
    branch_ref[0] = g_out.astype(BF)
    g_n2 = jnp.zeros((size, dim), F32)
    chunk = dim
    for start in range(0, hidden, chunk):
        cols = slice(start, start + chunk)
        g_hidden = dot_nt(branch_ref[0], wout_ref[cols, :])
        pre_ref[0, :, cols] = (g_hidden * dact_ref[0, :, cols].astype(F32)).astype(BF)
        g_n2 = g_n2 + dot_nt(pre_ref[0, :, cols], win_ref[:, cols])
    after = after_ref[0]
    scale = rms_scale(after)
    gain_2 = jnp.sum(g_n2 * after * scale, axis=0, keepdims=True)
    g_after = g_out + rms_back(after, scale, g_n2 * gain2_ref[...].astype(F32))
    gafter_ref[0] = g_after
    gmix_ref[0] = dot_nt(g_after.astype(BF), wo_ref[...]).astype(BF)

    @pl.when(row == 0)
    def _():
        gains_ref[...] = jnp.zeros_like(gains_ref)

    gains_ref[0:1, :] += gain_f
    gains_ref[1:2, :] += gain_2


def feed_back(lengths, place, block, after, cot, pool, dact, gains, weights):
    count, size, dim = block.shape
    slots = lengths.shape[1]
    hidden = dact.shape[2]
    outs = (
        ((size, dim), BF),
        ((size, hidden), BF),
        ((size, dim), F32),
        ((size, dim), BF),
    )
    constants = tuple(gains) + tuple(weights)
    return pl.pallas_call(
        feed_back_kernel,
        grid_spec=pltpu.PrefetchScalarGridSpec(
            num_scalar_prefetch=2,
            grid=(count,),
            in_specs=[row_spec((size, dim))] * 3
            + [row_spec((slots, dim)), row_spec((size, hidden))]
            + [full(item.shape) for item in constants],
            out_specs=[row_spec(shape) for shape, _ in outs]
            + [pl.BlockSpec((8, dim), lambda *_: (0, 0))],
        ),
        out_shape=[jax.ShapeDtypeStruct((count,) + shape, kind) for shape, kind in outs]
        + [jax.ShapeDtypeStruct((8, dim), F32)],
        compiler_params=params(),
        name="feed_back_rows",
    )(lengths, place, block, after, cot, pool, dact, *constants)


def weight_grad_kernel(left_ref, right_ref, out_ref):
    out_ref[...] = dot_tn(left_ref[...].astype(BF), right_ref[...].astype(BF)).astype(BF)


def weight_grad(left, right, tile):
    depth, rows = left.shape
    cols = right.shape[1]
    return pl.pallas_call(
        weight_grad_kernel,
        grid=(rows // tile,),
        in_specs=[
            pl.BlockSpec((depth, tile), lambda step: (0, step)),
            pl.BlockSpec((depth, cols), lambda step: (0, 0), pipeline_mode=pl.Buffered(1)),
        ],
        out_specs=pl.BlockSpec((tile, cols), lambda step: (step, 0)),
        out_shape=jax.ShapeDtypeStruct((rows, cols), BF),
        compiler_params=params(),
        name="weight_grad",
    )(left, right)


def attend_back_kernel(
    lengths_ref,
    place_ref,
    own_ref,
    low_ref,
    high_ref,
    q_ref,
    k_ref,
    v_ref,
    p_ref,
    gmix_ref,
    gafter_ref,
    gain1_ref,
    wq_ref,
    wk_ref,
    wv_ref,
    dq_ref,
    dk_ref,
    dv_ref,
    part_ref,
    halo_ref,
    acc_ref,
    gains_ref,
    mask_ref,
):
    size, dim = own_ref.shape[1:]
    heads = p_ref.shape[1]
    pairs = heads // 2
    lanes = dim // pairs
    row = pl.program_id(0)
    _, _, own, low, high = row_masks(lengths_ref, place_ref, row, size)
    mask_ref[0] = low.astype(BF)
    mask_ref[1] = own.astype(BF)
    mask_ref[2] = high.astype(BF)

    @pl.when(row == 0)
    def _():
        acc_ref[...] = jnp.zeros_like(acc_ref)
        gains_ref[...] = jnp.zeros_like(gains_ref)

    first_half = lax.broadcasted_iota(jnp.int32, (1, lanes), 1) < lanes // 2
    for pair in range(pairs):
        cols = slice(pair * lanes, (pair + 1) * lanes)
        q_pair = q_ref[0, :, cols]
        o_pair = gmix_ref[0, :, cols]
        zero = jnp.zeros_like(q_pair)
        d_q = []
        d_k = [None] * 3
        d_v = [None] * 3
        for half in range(2):
            head = 2 * pair + half
            keep = first_half if half == 0 else jnp.logical_not(first_half)
            q_head = jnp.where(keep, q_pair, zero)
            o_head = jnp.where(keep, o_pair, zero)
            own_on = mask_ref[1].astype(F32) > 0
            low_on = mask_ref[0].astype(F32) > 0
            g_low = dot_nt(o_head, v_ref[0, 0, :, cols])
            g_own = dot_nt(o_head, v_ref[0, 1, :, cols])
            g_high = dot_nt(o_head, v_ref[0, 2, :, cols])
            g_probs = jnp.where(own_on, g_own, jnp.where(low_on, g_low, g_high))
            probs = p_ref[0, head]
            wide = probs.astype(F32)
            product = wide * g_probs
            inner = jnp.sum(product, axis=-1, keepdims=True)
            g_scores = product - wide * inner
            on_own = jnp.where(own_on, g_scores, 0.0)
            acc_ref[head, :, :size] += on_own
            acc_ref[head, :, size:] += g_scores - on_own
            rounded = g_scores.astype(BF)
            total = None
            for part in range(3):
                piece = rounded * mask_ref[part]
                term = dot_nn(piece, k_ref[0, part, :, cols])
                total = term if total is None else total + term
                term = dot_tn(piece, q_head)
                d_k[part] = term if d_k[part] is None else d_k[part] + term
                term = dot_tn(probs * mask_ref[part], o_head)
                d_v[part] = term if d_v[part] is None else d_v[part] + term
            d_q.append(total)
        dq_ref[0, :, cols] = jnp.where(first_half, d_q[0], d_q[1]).astype(BF)
        for part in range(3):
            dk_ref[0, part, :, cols] = d_k[part].astype(BF)
            dv_ref[0, part, :, cols] = d_v[part].astype(BF)

    gain1 = gain1_ref[...].astype(F32)
    gain_1 = jnp.zeros((1, dim), F32)
    for part, source in enumerate((low_ref, own_ref, high_ref)):
        x = source[0].astype(F32)
        scale = rms_scale(x)
        g_norm = dot_nt(dk_ref[0, part], wk_ref[...]) + dot_nt(dv_ref[0, part], wv_ref[...])
        if part == 1:
            g_norm = g_norm + dot_nt(dq_ref[0], wq_ref[...])
        gain_1 = gain_1 + jnp.sum(g_norm * x * scale, axis=0, keepdims=True)
        g_x = rms_back(x, scale, g_norm * gain1)
        if part == 1:
            part_ref[0] = gafter_ref[0] + g_x
        else:
            halo_ref[0, part // 2] = g_x.astype(BF)
    gains_ref[0:1, :] += gain_1


def attend_back(lengths, place, own, low, high, q, k, v, p, gmix, gafter, gain1, weights):
    count, size, dim = own.shape
    heads = p.shape[1]
    outs = (
        ((size, dim), BF),
        ((3, size, dim), BF),
        ((3, size, dim), BF),
        ((size, dim), F32),
        ((2, size, dim), BF),
    )
    constants = (gain1,) + tuple(weights)
    return pl.pallas_call(
        attend_back_kernel,
        grid_spec=pltpu.PrefetchScalarGridSpec(
            num_scalar_prefetch=2,
            grid=(count,),
            in_specs=[row_spec((size, dim))] * 4
            + [row_spec((3, size, dim))] * 2
            + [row_spec((heads, size, size))]
            + [row_spec((size, dim))] * 2
            + [full(item.shape) for item in constants],
            out_specs=[row_spec(shape) for shape, _ in outs]
            + [
                pl.BlockSpec((heads, size, 2 * size), lambda *_: (0, 0, 0)),
                pl.BlockSpec((8, dim), lambda *_: (0, 0)),
            ],
            scratch_shapes=[pltpu.VMEM((3, size, size), BF)],
        ),
        out_shape=[jax.ShapeDtypeStruct((count,) + shape, kind) for shape, kind in outs]
        + [
            jax.ShapeDtypeStruct((heads, size, 2 * size), F32),
            jax.ShapeDtypeStruct((8, dim), F32),
        ],
        compiler_params=params(),
        name="attend_back_rows",
    )(lengths, place, own, low, high, q, k, v, p, gmix, gafter, *constants)


def flip(block, axis, bit):
    count = lax.axis_size(axis)
    return lax.ppermute(block, axis, [(i, i ^ bit) for i in range(count)])


def sum_along(block, axis):
    bit = 1
    while bit < lax.axis_size(axis):
        block = block + flip(block, axis, bit)
        bit *= 2
    return block


def gather_along(block, axis):
    bits = []
    bit = 1
    while bit < lax.axis_size(axis):
        bits.append(bit)
        bit *= 2
    place = lax.axis_index(axis)
    block = block[None]
    for bit in reversed(bits):
        other = flip(block, axis, bit)
        upper = (place // bit) % 2 == 1
        block = jnp.stack([jnp.where(upper, other, block), jnp.where(upper, block, other)], axis=1)
        block = block.reshape((-1,) + block.shape[2:])
    count = block.shape[0]
    order = []
    for index in range(count):
        where_at = 0
        for level, bit in enumerate(bits):
            if index & bit:
                where_at += count >> (level + 1)
        order.append(where_at)
    return jnp.concatenate([block[i] for i in order], axis=0)


def contrast(pooled, w_proj, partner):
    proj = w_proj.astype(F32)
    raw = jnp.dot(pooled, proj, precision=HIGHEST)
    inv_norm = lax.rsqrt(jnp.sum(raw * raw, axis=-1, keepdims=True) + EPS)
    embedded = raw * inv_norm
    everyone = lax.all_gather(embedded, "batch", axis=0, tiled=True)
    own_count = embedded.shape[0]
    total = everyone.shape[0]
    own_index = lax.axis_index("batch") * own_count + jnp.arange(own_count, dtype=jnp.int32)
    columns = jnp.arange(total, dtype=jnp.int32)

    def lse_of(rows, index):
        logits = SHARPNESS * jnp.einsum("nd,md->nm", rows, everyone, precision=HIGHEST)
        logits = jnp.where(columns[None, :] == index[:, None], NEGATIVE, logits)
        peak = jnp.max(logits, axis=-1, keepdims=True)
        return peak[:, 0] + jnp.log(jnp.sum(jnp.exp(logits - peak), axis=-1))

    if total <= 1024:
        lse_all = lse_of(everyone, columns)
    else:
        lse_all = lax.map(
            lambda pieces: lse_of(pieces[0], pieces[1]),
            (everyone.reshape(-1, 512, everyone.shape[1]), columns.reshape(-1, 512)),
        ).reshape(-1)
    logits = SHARPNESS * jnp.einsum("nd,md->nm", embedded, everyone, precision=HIGHEST)
    is_self = columns[None, :] == own_index[:, None]
    logits = jnp.where(is_self, NEGATIVE, logits)
    peak = jnp.max(logits, axis=-1, keepdims=True)
    lse_own = peak[:, 0] + jnp.log(jnp.sum(jnp.exp(logits - peak), axis=-1))
    is_target = columns[None, :] == partner[:, None]
    picked = jnp.sum(jnp.where(is_target, logits, 0.0), axis=-1)
    loss = lse_own - picked
    both = SHARPNESS * (
        jnp.exp(logits - lse_own[:, None])
        + jnp.exp(logits - lse_all[None, :])
        - 2.0 * is_target.astype(F32)
    )
    grad_emb = jnp.dot(both, everyone, precision=HIGHEST)
    grad_raw = inv_norm * (
        grad_emb - embedded * jnp.sum(embedded * grad_emb, axis=-1, keepdims=True)
    )
    grad_pooled = jnp.einsum("ne,de->nd", grad_raw, proj, precision=HIGHEST)
    return embedded, loss, grad_raw, grad_pooled


def shards(
    tokens,
    norm1_gain,
    w_query,
    w_key,
    w_value,
    rel_bias,
    w_output,
    norm2_gain,
    w_in,
    w_out,
    final_gain,
    w_proj,
    lengths,
    partner,
    cotangent,
):
    rows, size, dim = tokens.shape
    slots = lengths.shape[1]
    toks = rows * size
    seq_count = lax.axis_size("seq")
    seq_place = lax.axis_index("seq")
    place = seq_place.astype(jnp.int32).reshape(1)
    up = [(i, i + 1) for i in range(seq_count - 1)]
    down = [(i + 1, i) for i in range(seq_count - 1)]
    gain1 = norm1_gain.reshape(1, dim)
    gain2 = norm2_gain.reshape(1, dim)
    gainf = final_gain.reshape(1, dim)

    x_low = lax.ppermute(tokens, "seq", up)
    x_high = lax.ppermute(tokens, "seq", down)
    bias = bias_tables(rel_bias, size)
    (block, partial, n1, q, k, v, p, att, after, n2, act, dact) = forward(
        0,
        rows,
        lengths,
        place,
        tokens,
        x_low,
        x_high,
        (gain1, gain2, gainf),
        (w_query, w_key, w_value, w_output, w_in, w_out),
        bias,
    )
    pooled_sum = sum_along(partial, "seq")
    counts = lengths.astype(F32)[:, :, None]
    pooled = (pooled_sum / counts).reshape(rows * slots, dim)
    embedded, loss, grad_raw, grad_pooled = contrast(pooled, w_proj, partner)
    lead_only = (seq_place == 0).astype(F32)
    grad_proj = jnp.einsum("ne,nd->ed", lead_only * grad_raw, pooled, precision=HIGHEST)
    pool_grad = grad_pooled.reshape(rows, slots, dim) / counts

    g_branch, g_pre, g_after, g_mix, gains_a = feed_back(
        lengths,
        place,
        block,
        after,
        cotangent,
        pool_grad,
        dact,
        (gain2, gainf),
        (w_output, w_in, w_out),
    )
    flat = lambda array: array.reshape(-1, array.shape[-1])
    t_in = weight_grad(flat(g_pre), flat(n2), 768)
    t_out = weight_grad(flat(g_branch), flat(act), 256)
    t_output = weight_grad(flat(g_after), flat(att), 768)
    dq, dk, dv, part, halo, acc, gains_b = attend_back(
        lengths,
        place,
        tokens,
        x_low,
        x_high,
        q,
        k,
        v,
        p,
        g_mix,
        g_after,
        gain1,
        (w_query, w_key, w_value),
    )
    from_above = lax.ppermute(halo[:, 0], "seq", down)
    from_below = lax.ppermute(halo[:, 1], "seq", up)
    t_query = weight_grad(flat(dq), flat(n1[:, 1]), 768)
    t_key = weight_grad(flat(dk), flat(n1), 768)
    t_value = weight_grad(flat(dv), flat(n1), 768)
    grad_tokens = part + from_above.astype(F32) + from_below.astype(F32)
    grad_rel = bias_grad(acc, rel_bias.shape[0])

    batch_count = lax.axis_size("batch")

    def reduce(array):
        return lax.psum_scatter(array, "batch", scatter_dimension=0, tiled=True)

    def finish(array):
        mine = lax.psum_scatter(array, "seq", scatter_dimension=1, tiled=True)
        return mine.T.astype(F32)

    s_in = finish(reduce(t_in))
    s_out = finish(reduce(t_out))
    small = [
        finish(reduce(item.astype(BF)))
        for item in (t_query, t_key, t_value, t_output, grad_proj)
    ]
    sums = lax.psum((gains_b[0], gains_a[1], gains_a[0], grad_rel), ("batch", "seq"))
    return (
        block,
        embedded,
        loss,
        grad_tokens,
        sums[0],
        small[0],
        small[1],
        small[2],
        sums[3],
        small[3],
        sums[1],
        s_in,
        s_out,
        sums[2],
        small[4],
    )


def solution(mesh):
    tok = P("batch", "seq", None)
    mat = P("seq", "batch")
    return jax.shard_map(
        shards,
        mesh=mesh,
        in_specs=(tok,) + (P(),) * 11 + (P("batch", None), P("batch"), tok),
        out_specs=(
            tok,
            P("batch", None),
            P("batch"),
            tok,
            P(),
            mat,
            mat,
            mat,
            P(),
            mat,
            P(),
            mat,
            mat,
            P(),
            mat,
        ),
        check_vma=False,
    )
```

time: 1080 us -> 660 us (0.61)
  matrix products: 308 us -> 12.8 us
  Pallas kernels: 0 us -> 194 us
  other arithmetic: 134 us -> 9.71 us
  waiting for transfers between devices: 439 us -> 323 us
  local copies, waits for them, and re-layouts: 122 us -> 36.3 us
    dot_general x42 -> x6, matrix products: 308 us -> 12.8 us  [the longest x1 4.69 us: lse_of(): jnp.einsum('nd,md->nm', rows, everyone, precision=HIGHEST)]
    pallas_call x0 -> x11, Pallas kernels: none -> 194 us  [the longest x1 62.2 us: forward(): pl.pallas_call(functools.partial(forward_kernel, first), grid_spec=pltpu....]
    reduce_scatter x10 -> x8, waiting for transfers between devices: 247 us -> 160 us  [the longest x7 140 us: reduce(): return lax.psum_scatter(array, 'batch', scatter_dimension=0, tiled=True)]
    reduce_sum x10 -> x2, other arithmetic: 81.6 us -> 0.41 us  [the longest x1 0.21 us: contrast(): picked = jnp.sum(jnp.where(is_target, logits, 0.0), axis=-1)]
    unnamed x22 -> x21, waiting for transfers between devices: 41.6 us -> 97.5 us
    ppermute x4 -> x6, waiting for transfers between devices: 86.4 us -> 39.9 us  [the longest x1 24.4 us: shards(): x_low = lax.ppermute(tokens, 'seq', up)]
    psum x1 -> x0, waiting for transfers between devices: 38.8 us -> none  [shards(): pooled_sum = lax.psum(partial_sums, 'seq')]
    dynamic_update_slice x6 -> x0, local copies, waits for them, and re-layouts: 24.9 us -> none  [the longest x2 17.1 us: shards(): lax.map(backward_block, (blocks_q, back_k, back_v, blocks_mask, blocks_gr...]
  transfers between devices with their start and end apart: 21 -> 21, of which waited for: 16 -> 15; matrix products, arithmetic and copies ran while one was open for 36% -> 7% of each run, Pallas kernels for 0% -> 20%
where the time goes in v1:
time: 660 us; the launch traced here: 649 us
  waiting for transfers between devices  323 us (49%)
  Pallas kernels  194 us (29%)
  blocking collectives  40.2 us (6%)
  local copies, waits for them, and re-layouts  36.3 us (5%)
  starting transfers between devices  18.9 us (3%)
  between operations  14.7 us (2%)
  matrix products  12.8 us (2%)
  other arithmetic  9.71 us (1%)
    reduce_scatter x7, waiting for transfers between devices, reduce(): return lax.psum_scatter(array, 'batch', scatter_dimension=0, tiled=True)  140 us
    unnamed x21, waiting for transfers between devices  97.5 us
    pallas_call x1, Pallas kernels, forward(): pl.pallas_call(functools.partial(forward_kernel, first), grid_spec=pltpu....  62.2 us
    pallas_call x1, Pallas kernels, attend_back(): pl.pallas_call(attend_back_kernel, grid_spec=pltpu.PrefetchScalarGridSpec...  51.3 us
    pallas_call x6, Pallas kernels, weight_grad(): pl.pallas_call(weight_grad_kernel, grid=(rows // tile,), in_specs=[pl.Blo...  45.4 us
    psum x1, blocking collectives, shards(): lax.psum((gains_b[0], gains_a[1], gains_a[0], grad_rel), ('batch', 'seq'))  40.2 us
    pallas_call x1, Pallas kernels, feed_back(): pl.pallas_call(feed_back_kernel, grid_spec=pltpu.PrefetchScalarGridSpec(n...  25.6 us
    all_gather x1, waiting for transfers between devices, contrast(): everyone = lax.all_gather(embedded, 'batch', axis=0, tiled=True)  25.3 us
  transfers between devices with their start and end apart: 21, of which 15 were waited for; matrix products, arithmetic and copies ran while one was open for 7% of the time, Pallas kernels for 20%

profile of v1, /device:TPU:0, one launch (start us, length us, event | category | flops | bytes accessed | tf_op | source)
XLA Modules:
  0.0 649.4 jit_solution(13632685250891610178)
XLA Ops:
  7.2 5.2 collective-permute-start
  18.9 3.0 shard_map.262.bias_ref
  21.9 24.4 %collective-permute-done.low_ref = bf16[4,256,768]{2,1,0:T(8,128)(2,1)S(1)} collective-permute-done((bf16[4,256,768]{2,1,0:T(8,128)(2,1)}, bf16[4,256,768]{2,1,0:T(8,128)(2,1)S(1)}, u32[]{:S(2)}, u32[]{:S(2)}) %collective-permute-start) | collective-permute-done | bytes 1572896 | tf_op jit(solution)/shard_map/ppermute | solution.py:655
  46.3 4.2 collective-permute-done.1.high_ref
  50.5 62.2 %forward_rows.1 = (bf16[4,256,768]{2,1,0:T(8,128)(2,1)}, f32[4,16,768]{2,1,0:T(8,128)}, bf16[4,3,256,768]{3,2,1,0:T(8,128)(2,1)}, bf16[4,256,768]{2,1,0:T(8,128)...) custom-call(s32[4,16]{1,0:T(4,128)} %lengths_ref.5, ...), custom_call_target="tpu_custom_call" | custom-call | tf_op jit(solution)/shard_map/forward_rows/pallas_call | solution.py:278
  114.3 4.4 collective-permute-done.2
  122.1 6.9 %collective-permute-done.3 = f32[4,16,768]{2,1,0:T(8,128)S(1)} collective-permute-done((f32[4,16,768]{2,1,0:T(8,128)S(1)}, f32[4,16,768]{2,1,0:T(8,128)S(1)}, u32[]{:S(2)}, u32[]{:S(2)}) %collective-permute-start.3) | collective-permute-done | bytes 196640 | tf_op jit(solution)/shard_map/ppermute | solution.py:546
  131.2 25.3 %all-gather.2.cloned.1.call-done = f32[512,768]{1,0:T(8,128)} async-done(((f32[64,768]{1,0:T(8,128)}), f32[512,768]{1,0:T(8,128)}) %all-gather.2.cloned.1.call-update) | async-done | bytes 1572880 | tf_op jit(solution)/shard_map/all_gather | solution.py:586
  156.5 4.7 fusion.25
  165.1 3.2 convolution_convert_fusion
  170.4 25.6 %feed_back_rows.1 = (bf16[4,256,768]{2,1,0:T(8,128)(2,1)}, bf16[4,256,3072]{2,1,0:T(8,128)(2,1)}, f32[4,256,768]{2,1,0:T(8,128)}, bf16[4,256,768]{2,1,0:T(8,128)(2,1)}, f32[8,768]{1,0:T(8,128)}) custom-call(s32[4,16]{1,0:T(4,128)} %lengths_ref.5, s32[1]{0:T(128)} %bitcast.place_ref, bf16[4,256,768]{2,1,0:T(8,128)(2,1)} %get-tuple-element.78.block_ref, ...), custom_call_target="tpu_custom_call" | custom-call | tf_op jit(solution)/shard_map/feed_back_rows/pallas_call | solution.py:366
  196.0 4.8 weight_grad.9
  201.0 51.3 %attend_back_rows.1 = (bf16[4,256,768]{2,1,0:T(8,128)(2,1)}, bf16[4,3,256,768]{3,2,1,0:T(8,128)(2,1)}, bf16[4,3,256,768]{3,2,1,0:T(8,128)(2,1)}, f32[4,256,768]{...) custom-call(s32[4,16]{1,0:T(4,128)} %lengths_ref.5, ...), custom_call_target="tpu_custom_call" | custom-call | tf_op jit(solution)/shard_map/attend_back_rows/pallas_call | solution.py:517
  252.4 8.7 %weight_grad.8 = bf16[768,768]{1,0:T(8,128)(2,1)} custom-call(bf16[3072,768]{1,0:T(8,128)(2,1)} %bitcast.60, bf16[3072,768]{1,0:T(8,128)(2,1)} %bitcast.53), custom_call_target="tpu_custom_call" | custom-call | tf_op jit(solution)/shard_map/weight_grad/pallas_call | solution.py:391
  261.1 8.6 %weight_grad.7 = bf16[768,768]{1,0:T(8,128)(2,1)} custom-call(bf16[3072,768]{1,0:T(8,128)(2,1)} %bitcast.59, bf16[3072,768]{1,0:T(8,128)(2,1)} %bitcast.54), custom_call_target="tpu_custom_call" | custom-call | tf_op jit(solution)/shard_map/weight_grad/pallas_call | solution.py:391
  272.5 4.4 weight_grad.6
  277.0 9.2 %weight_grad.10 = bf16[3072,768]{1,0:T(8,128)(2,1)} custom-call(bf16[1024,3072]{1,0:T(8,128)(2,1)} %bitcast.57, bf16[1024,768]{1,0:T(8,128)(2,1)} %bitcast.64), custom_call_target="tpu_custom_call" | custom-call | tf_op jit(solution)/shard_map/weight_grad/pallas_call | solution.py:391
  288.2 9.7 %weight_grad.11 = bf16[768,3072]{1,0:T(8,128)(2,1)} custom-call(bf16[1024,768]{1,0:T(8,128)(2,1)} %bitcast.65, bf16[1024,3072]{1,0:T(8,128)(2,1)} %bitcast.56), custom_call_target="tpu_custom_call" | custom-call | tf_op jit(solution)/shard_map/weight_grad/pallas_call | solution.py:391
  308.2 5.7 collective-permute-start.5
  313.9 24.3 %reduce-scatter.29.cloned.1.call-done = bf16[96,768]{1,0:T(8,128)(2,1)} async-done(((bf16[768,768]{1,0:T(8,128)(2,1)}), bf16[96,768]{1,0:T(8,128)(2,1)}) %reduce-scatter.29.cloned.1.call-update) | async-done | bytes 147472 | tf_op jit(solution)/shard_map/reduce_scatter | solution.py:719
  340.0 38.1 %reduce-scatter.27.cloned.1.call-done = bf16[96,768]{1,0:T(8,128)(2,1)} async-done(((bf16[768,768]{1,0:T(8,128)(2,1)}), bf16[96,768]{1,0:T(8,128)(2,1)}) %reduce-scatter.27.cloned.1.call-update) | async-done | bytes 147472 | tf_op jit(solution)/shard_map/reduce_scatter | solution.py:719
  379.9 55.9 %reduce-scatter.35.cloned.1.call-done = bf16[384,768]{1,0:T(8,128)(2,1)} async-done(((bf16[3072,768]{1,0:T(8,128)(2,1)}), bf16[384,768]{1,0:T(8,128)(2,1)}) %reduce-scatter.35.cloned.1.call-update) | async-done | bytes 589840 | tf_op jit(solution)/shard_map/reduce_scatter | solution.py:719
  438.3 6.3 shard_map.263
  446.2 40.2 %all-reduce = (f32[768]{0:T(1024)}, f32[32,12]{1,0:T(8,128)S(1)}, f32[768]{0:T(1024)}, f32[768]{0:T(1024)}) all-reduce(f32[768]{0:T(1024)S(1)} %slice_reduce_fusion.2, f32[32,12]{1,0:T(8,128)} %shard_map.263, f32[768]{0:T(1024)S(1)} %get-tuple-element.96, ...), channel_id=1, replica_groups=mesh['batch'=8,'seq'=4] {'batch','seq'}, use_global_device_ids=true, to_apply=%region_7.8 | all-reduce | flops 2688 | bytes 21504 | tf_op jit(solution)/shard_map/psum | solution.py:731
  487.1 4.5 convert_add_fusion
  492.5 21.2 %reduce-scatter.37.cloned.1.call-done = bf16[96,3072]{1,0:T(8,128)(2,1)} async-done(((bf16[768,3072]{1,0:T(8,128)(2,1)}), bf16[96,3072]{1,0:T(8,128)(2,1)}) %reduce-scatter.37.cloned.1.call-update) | async-done | bytes 589840 | tf_op jit(solution)/shard_map/reduce_scatter | solution.py:719
  514.4 20.7 %reduce-scatter.49.cloned.1.call-done = bf16[192,96]{1,0:T(8,128)(2,1)} async-done(((bf16[768,96]{1,0:T(8,128)(2,1)}), bf16[192,96]{1,0:T(8,128)(2,1)}) %reduce-scatter.49.cloned.1.call-update) | async-done | bytes 36880
  536.8 18.3 %reduce-scatter.47.cloned.1.call-done = bf16[192,96]{1,0:T(8,128)(2,1)} async-done(((bf16[768,96]{1,0:T(8,128)(2,1)}), bf16[192,96]{1,0:T(8,128)(2,1)}) %reduce-scatter.47.cloned.1.call-update) | async-done | bytes 36880
  556.8 18.6 %reduce-scatter.45.cloned.1.call-done = bf16[192,96]{1,0:T(8,128)(2,1)} async-done(((bf16[768,96]{1,0:T(8,128)(2,1)}), bf16[192,96]{1,0:T(8,128)(2,1)}) %reduce-scatter.45.cloned.1.call-update) | async-done | bytes 36880
  577.0 18.9 %reduce-scatter.43.cloned.1.call-done = bf16[192,96]{1,0:T(8,128)(2,1)} async-done(((bf16[768,96]{1,0:T(8,128)(2,1)}), bf16[192,96]{1,0:T(8,128)(2,1)}) %reduce-scatter.43.cloned.1.call-update) | async-done | bytes 36880
  597.6 20.7 %reduce-scatter.51.cloned.1.call-done = bf16[192,384]{1,0:T(8,128)(2,1)} async-done(((bf16[768,384]{1,0:T(8,128)(2,1)}), bf16[192,384]{1,0:T(8,128)(2,1)}) %reduce-scatter.51.cloned.1.call-update) | async-done | bytes 147472
  620.2 20.5 %reduce-scatter.39.cloned.1.call-done = bf16[96,768]{1,0:T(8,128)(2,1)} async-done(((bf16[96,3072]{1,0:T(8,128)(2,1)}), bf16[96,768]{1,0:T(8,128)(2,1)}) %reduce-scatter.39.cloned.1.call-update) | async-done | bytes 147472 | tf_op jit(solution)/shard_map/reduce_scatter | solution.py:722
  (104 shorter events, 54.9 us)
Async XLA Ops:
  7.2 122.0 %copy-start = (bf16[768,768]{1,0:T(8,128)(2,1)S(1)}, bf16[768,768]{1,0:T(8,128)(2,1)}, u32[]{:S(2)}) copy-start(bf16[768,768]{1,0:T(8,128)(2,1)} %param.26) | copy-start | bytes 3538948
  7.2 149.3 %all-gather.2.cloned.1.call-start = ((), (), s32[]{:S(2)}) async-start(), calls=%async_computation.14 | async-start | bytes 1769472 | tf_op jit(solution)/shard_map/all_gather | solution.py:586
  7.2 39.0 %collective-permute-start = (bf16[4,256,768]{2,1,0:T(8,128)(2,1)}, bf16[4,256,768]{2,1,0:T(8,128)(2,1)S(1)}, u32[]{:S(2)}, u32[]{:S(2)}) collective-permute-start(bf16[4,256,768]{2,1,0:T(8,128)(2,1)} %own_ref.3), channel_id=1, source_target_pairs={{0,1},{1,2},{2,3},{4,5},{5,6},{6,7},{8,9},{9,10},{10,11},{12,13},{... | collective-permute-start | bytes 4718600 | tf_op jit(solution)/shard_map/ppermute | solution.py:655
  12.4 38.1 %collective-permute-start.1 = (bf16[4,256,768]{2,1,0:T(8,128)(2,1)}, bf16[4,256,768]{2,1,0:T(8,128)(2,1)}, u32[]{:S(2)}, u32[]{:S(2)}) collective-permute-start(bf16[4,256,768]{2,1,0:T(8,128)(2,1)} %own_ref.3), channel_id=1, source_target_pairs={{1,0},{2,1},{3,2},{5,4},{6,5},{7,6},{9,8},{10,9},{11,10},{13,12},{... | collective-permute-start | bytes 4718600 | tf_op jit(solution)/shard_map/ppermute | solution.py:656
  46.3 4.2 copy-start.4
  50.5 71.7 %copy-start.5 = (s32[4,16]{1,0:T(4,128)S(1)}, s32[4,16]{1,0:T(4,128)}, u32[]{:S(2)}) copy-start(s32[4,16]{1,0:T(4,128)} %lengths_ref.5) | copy-start | bytes 772
  112.7 5.9 collective-permute-start.2
  119.6 9.5 %collective-permute-start.3 = (f32[4,16,768]{2,1,0:T(8,128)S(1)}, f32[4,16,768]{2,1,0:T(8,128)S(1)}, u32[]{:S(2)}, u32[]{:S(2)}) collective-permute-start(f32[4,16,768]{2,1,0:T(8,128)S(1)} %add.86), channel_id=1, source_target_pairs={{0,2},{1,3},{2,0},{3,1},{4,6},{5,7},{6,4},{7,5},{8,10},{9,11},{10,... | collective-permute-start | bytes 589832 | tf_op jit(solution)/shard_map/ppermute | solution.py:546
  130.8 155.6 %reduce-scatter.41.cloned.1.call-start = ((), (), s32[]{:S(2)}) async-start(), calls=%async_computation.22 | async-start | bytes 1327104 | tf_op jit(solution)/shard_map/reduce_scatter | solution.py:719
  131.2 30.2 %copy-start.3 = (f32[64,768]{1,0:T(8,128)S(1)}, f32[64,768]{1,0:T(8,128)}, u32[]{:S(2)}) copy-start(f32[64,768]{1,0:T(8,128)} %broadcast_multiply_fusion) | copy-start | bytes 589828
  156.5 4.9 copy-start.2
  161.2 2.0 copy-start.6
  168.3 129.6 %reduce-scatter.33.cloned.1.call-start = ((), (), s32[]{:S(2)}) async-start(), calls=%async_computation.18 | async-start | bytes 1327104 | tf_op jit(solution)/shard_map/reduce_scatter | solution.py:719
  200.8 101.6 %reduce-scatter.31.cloned.1.call-start = ((), (), s32[]{:S(2)}) async-start(), calls=%async_computation.17 | async-start | bytes 1327104 | tf_op jit(solution)/shard_map/reduce_scatter | solution.py:719
  261.1 77.1 %reduce-scatter.29.cloned.1.call-start = ((), (), s32[]{:S(2)}) async-start(), calls=%async_computation.16 | async-start | bytes 1327104 | tf_op jit(solution)/shard_map/reduce_scatter | solution.py:719
  269.8 108.3 %reduce-scatter.27.cloned.1.call-start = ((), (), s32[]{:S(2)}) async-start(), calls=%async_computation.15 | async-start | bytes 1327104 | tf_op jit(solution)/shard_map/reduce_scatter | solution.py:719
  277.0 158.8 %reduce-scatter.35.cloned.1.call-start = ((), (), s32[]{:S(2)}) async-start(), calls=%async_computation.19 | async-start | bytes 5308416 | tf_op jit(solution)/shard_map/reduce_scatter | solution.py:719
  286.3 205.3 %reduce-scatter.53.cloned.1.call-start = ((), (), s32[]{:S(2)}) async-start(), calls=%async_computation.28 | async-start | bytes 245760
  288.1 225.5 %reduce-scatter.37.cloned.1.call-start = ((), (), s32[]{:S(2)}) async-start(), calls=%async_computation.20 | async-start | bytes 5308416 | tf_op jit(solution)/shard_map/reduce_scatter | solution.py:719
  297.9 237.3 %reduce-scatter.49.cloned.1.call-start = ((), (), s32[]{:S(2)}) async-start(), calls=%async_computation.26 | async-start | bytes 245760
  299.7 255.4 %reduce-scatter.47.cloned.1.call-start = ((), (), s32[]{:S(2)}) async-start(), calls=%async_computation.25 | async-start | bytes 245760
  304.2 271.2 %reduce-scatter.45.cloned.1.call-start = ((), (), s32[]{:S(2)}) async-start(), calls=%async_computation.24 | async-start | bytes 245760
  306.9 180.2 %collective-permute-start.4 = (bf16[4,256,768]{2,1,0:T(8,128)(2,1)}, bf16[4,256,768]{2,1,0:T(8,128)(2,1)S(1)}, u32[]{:S(2)}, u32[]{:S(2)}) collective-permute-start(bf16[4,256,768]{2,1,0:T(8,128)(2,1)} %slice_bitcast_fusion), channel_id=1, source_target_pairs={{1,0},{2,1},{3,2},{5,4},{6,5},{7,6},{9,8},{10,9},{11,10},{13,12},{... | collective-permute-start | bytes 4718600 | tf_op jit(solution)/shard_map/ppermute | solution.py:708
  308.2 178.9 %collective-permute-start.5 = (bf16[4,256,768]{2,1,0:T(8,128)(2,1)}, bf16[4,256,768]{2,1,0:T(8,128)(2,1)}, u32[]{:S(2)}, u32[]{:S(2)}) collective-permute-start(bf16[4,256,768]{2,1,0:T(8,128)(2,1)} %slice_bitcast_fusion.1), channel_id=1, source_target_pairs={{0,1},{1,2},{2,3},{4,5},{5,6},{6,7},{8,9},{9,10},{10,11},{12,13},{... | collective-permute-start | bytes 4718600 | tf_op jit(solution)/shard_map/ppermute | solution.py:709
  339.9 256.0 %reduce-scatter.43.cloned.1.call-start = ((), (), s32[]{:S(2)}) async-start(), calls=%async_computation.23 | async-start | bytes 245760
  379.8 238.5 %reduce-scatter.51.cloned.1.call-start = ((), (), s32[]{:S(2)}) async-start(), calls=%async_computation.27 | async-start | bytes 737280
  438.0 202.8 %reduce-scatter.39.cloned.1.call-start = ((), (), s32[]{:S(2)}) async-start(), calls=%async_computation.21 | async-start | bytes 737280 | tf_op jit(solution)/shard_map/reduce_scatter | solution.py:722
  556.0 86.4 %copy-start.1 = (bf16[768,768]{1,0:T(8,128)(2,1)S(1)}, bf16[768,768]{1,0:T(8,128)(2,1)}, u32[]{:S(2)}) copy-start(bf16[768,768]{1,0:T(8,128)(2,1)} %param.26) | copy-start | bytes 3538948
Sparse Core Ops, SparseCore 0:
  130.9 25.5 all-gather.1
  168.4 36.7 reduce-scatter.40
  208.8 36.7 reduce-scatter.32
  261.2 36.7 reduce-scatter.30
  301.4 36.7 reduce-scatter.28
  341.3 36.7 reduce-scatter.26
  381.9 53.8 reduce-scatter.34
  438.1 19.2 reduce-scatter.52
  461.2 52.3 reduce-scatter.36
  515.7 19.3 reduce-scatter.48
  537.5 17.5 reduce-scatter.46
  557.8 17.5 reduce-scatter.44
  578.3 17.5 reduce-scatter.42
  598.0 20.1 reduce-scatter.50
  620.4 20.3 reduce-scatter.38
